TPU v7x, 32 devices: a whole 2x2x4 slice. The times are simulated.
32 devices in a mesh: ctx: 8 (over y, x, core), exp: 4 (over z).
Axes of the slice: x: 2, y: 2, z: 4, core: 2. Of those that a mesh axis runs over, the one named last changes fastest.
Arguments:
- latent: bfloat16 [1024, 576], P('ctx'), may hold values from -8 to 8
- query: bfloat16 [1024, 12288], P('ctx', 'exp'), may hold values from -8 to 8
- w_uk: bfloat16 [64, 512, 128], P('exp'), may hold values from -0.5 to 0.5
- w_uv: bfloat16 [64, 512, 128], P('exp'), may hold values from -0.25 to 0.25
- w_o: bfloat16 [8192, 4096], P('exp'), may hold values from -0.0625 to 0.0625
- residual: bfloat16 [1024, 4096], P('ctx', 'exp'), may hold values from -16 to 16
- norm_gain: float32 [4096], P('exp'), may hold values from 0.1 to 1.9
- w_in: bfloat16 [16, 4096, 2, 2048], P('ctx', None, None, 'exp'), may hold values from -0.09375 to 0.09375
- w_out: bfloat16 [16, 2048, 4096], P('ctx', 'exp'), may hold values from -0.125 to 0.125
- routes: int32 [1024, 8], P('ctx'), may hold values from 0 to 15, all different within a row; in each aligned block of 128 rows (0 to 127, 128 to 255, ...) at most 96 rows name the same one
- gate_weights: float32 [1024, 8], P('ctx'), may hold values from 0.05 to 0.5
- doc_lengths: int32 [12], replicated, may hold values from 1 to 640, 1024 in all
Outputs:
- mixed: bfloat16 [1024, 4096], P('ctx', 'exp')
Inputs may be any that keep to these rules, and one draw needn't show every extreme that they name: `routes`: the 128 rows of one index of ctx name each expert at most 96 times in all, a bound that some block reaches.
All inputs are finite; a program needn't handle non-finite values.
Results may differ from a plain program's by a relative error of at most 0.009.
Values may be sent and summed in bfloat16 or wider, within the bound.
A program may use at most 128 MiB of HBM per device.

v0:
```python
import math

import jax
import jax.numpy as jnp
from jax import lax
from jax.sharding import PartitionSpec as P

D = 4096
NOPE = 128
ROPE = 64
LAT = 512
VDIM = 128
TOP = 8


epsilon = 1e-06


def document(positions, doc_ends):
    return jnp.sum((positions[:, None] >= doc_ends[None, :]).astype(jnp.int32), axis=1)


def expert_mlp(arrived, w_in, w_out, local_experts, capacity):
    sources = arrived.shape[0]
    grouped = arrived.reshape(sources, local_experts, capacity, arrived.shape[2])
    hidden_pre = jnp.einsum("secd,edgf->secgf", grouped, w_in, preferred_element_type=jnp.float32)
    activated = (jax.nn.silu(hidden_pre[:, :, :, 0, :]) * hidden_pre[:, :, :, 1, :]).astype(
        jnp.bfloat16
    )
    partials = jnp.einsum(
        "secf,efd->secd", activated, w_out, preferred_element_type=jnp.float32
    ).astype(jnp.bfloat16)
    return partials.reshape(sources, local_experts * capacity, w_out.shape[2])


def body(
    latent,
    query,
    w_uk,
    w_uv,
    w_o,
    residual,
    norm_gain,
    w_in,
    w_out,
    routes,
    gate_weights,
    doc_lengths,
):
    count_ctx = lax.axis_size("ctx")
    tokens = latent.shape[0]
    heads = w_uk.shape[0]
    qk_width = NOPE + ROPE
    score_scale = 1.0 / math.sqrt(qk_width)
    doc_ends = jnp.cumsum(doc_lengths)
    first_pos = lax.axis_index("ctx") * tokens
    q_pos = first_pos + jnp.arange(tokens, dtype=jnp.int32)
    q_doc = document(q_pos, doc_ends)
    q_rows = query.reshape(tokens, heads, qk_width)
    q_lat = jnp.einsum(
        "thn,hln->htl", q_rows[:, :, :NOPE], w_uk, preferred_element_type=jnp.float32
    ).astype(jnp.bfloat16)
    q_full = jnp.concatenate(
        [q_lat, jnp.transpose(q_rows[:, :, NOPE:], (1, 0, 2))], axis=2
    ).reshape(heads * tokens, LAT + ROPE)
    row_pos = jnp.tile(q_pos, heads)
    row_doc = jnp.tile(q_doc, heads)
    row_count = heads * tokens
    piece = lax.all_gather(latent, "ctx", axis=0, tiled=True)
    key_pos = jnp.arange(piece.shape[0], dtype=jnp.int32)
    key_doc = document(key_pos, doc_ends)
    allowed = (row_doc[:, None] == key_doc[None, :]) & (row_pos[:, None] >= key_pos[None, :])
    row_max = jnp.full((row_count,), -1e30, jnp.float32)
    scores = jnp.dot(q_full, piece.T, preferred_element_type=jnp.float32) * score_scale
    scores = jnp.where(allowed, scores, -1e30)
    new_max = jnp.maximum(row_max, jnp.max(scores, axis=1))
    weights = jnp.where(allowed, jnp.exp(scores - new_max[:, None]), 0.0)
    row_total = jnp.sum(weights, axis=1)
    accumulated = jnp.dot(
        weights.astype(jnp.bfloat16), piece[:, :LAT], preferred_element_type=jnp.float32
    )
    row_max, row_total, accumulated = (new_max, row_total, accumulated)
    o_lat = (accumulated / row_total[:, None]).astype(jnp.bfloat16).reshape(heads, tokens, LAT)
    head_out = (
        jnp.einsum("htl,hlv->thv", o_lat, w_uv, preferred_element_type=jnp.float32)
        .astype(jnp.bfloat16)
        .reshape(tokens, heads * VDIM)
    )
    local_width = residual.shape[1]
    attn_t = lax.psum_scatter(
        lax.dot_general(
            w_o, head_out, (((0,), (1,)), ((), ())), preferred_element_type=jnp.float32
        ).astype(jnp.bfloat16),
        "exp",
        scatter_dimension=0,
        tiled=True,
    ).astype(jnp.float32)
    hidden = residual.astype(jnp.float32) + attn_t.T
    squares = lax.psum(jnp.sum(hidden * hidden, axis=1), "exp")
    normed = (hidden * lax.rsqrt(squares[:, None] / D + epsilon) * norm_gain[None, :]).astype(
        jnp.bfloat16
    )
    local_experts = w_in.shape[0]
    experts = local_experts * count_ctx
    capacity = tokens * TOP * 3 // (2 * experts)
    flat_routes = routes.reshape(-1)
    onehot = (flat_routes[:, None] == jnp.arange(experts, dtype=jnp.int32)[None, :]).astype(
        jnp.int32
    )
    slot_rank = jnp.sum((jnp.cumsum(onehot, axis=0) - onehot) * onehot, axis=1)
    slot_index = flat_routes * capacity + slot_rank
    owner_row = (
        jnp.zeros((experts * capacity,), jnp.int32)
        .at[slot_index]
        .set(jnp.arange(tokens * TOP, dtype=jnp.int32) // TOP)
    )
    filled = jnp.zeros((experts * capacity,), jnp.bool_).at[slot_index].set(True)
    gate_flat = gate_weights.reshape(-1)
    outgoing = jnp.where(filled[:, None], normed[owner_row], jnp.zeros((), jnp.bfloat16)).reshape(
        count_ctx, local_experts * capacity, local_width
    )
    arrived = lax.all_to_all(outgoing, "ctx", split_axis=0, concat_axis=0, tiled=True)
    rows_full = lax.all_gather(arrived, "exp", axis=2, tiled=True)
    partials = expert_mlp(rows_full, w_in, w_out, local_experts, capacity)
    summed = lax.psum_scatter(partials, "exp", scatter_dimension=2, tiled=True).astype(jnp.float32)
    returned = (
        lax.all_to_all(summed.astype(jnp.bfloat16), "ctx", split_axis=0, concat_axis=0, tiled=True)
        .astype(summed.dtype)
        .reshape(experts * capacity, local_width)
    )
    picked = returned[slot_index] * gate_flat[:, None]
    moe_out = jnp.sum(picked.reshape(tokens, TOP, local_width), axis=1)
    return (hidden + moe_out).astype(jnp.bfloat16)


def solution(mesh):
    placed = (
        P("ctx", None),
        P("ctx", "exp"),
        P("exp", None, None),
        P("exp", None, None),
        P("exp", None),
        P("ctx", "exp"),
        P("exp"),
        P("ctx", None, None, "exp"),
        P("ctx", "exp", None),
        P("ctx", None),
        P("ctx", None),
        P(),
    )
    return jax.shard_map(
        body, mesh=mesh, in_specs=placed, out_specs=P("ctx", "exp"), check_vma=False
    )
```

profile of v0, /device:TPU:0, one launch (start us, length us, event | category | flops | bytes accessed | tf_op | source)
XLA Modules:
  0.0 682.0 jit_solution(15871963575645133259)
XLA Ops:
  6.5 0.0 copy-start
  6.5 0.0 all-gather.3.cloned.1.call-start
  6.5 0.7 all-gather.3.cloned.1.call-update
  7.3 0.0 reduce-scatter.3.cloned.1.call-start
  7.3 1.5 copy.33
  8.8 0.7 slice.33
  9.5 1.2 copy.56
  10.8 0.8 reduce-window.18
  11.6 0.1 convert_reduce_fusion
  11.7 0.1 convert_reduce_fusion.1
  11.8 0.0 copy-done
  11.8 0.8 convolution_convert_fusion.1
  12.6 1.8 pad_maximum_fusion
  14.4 21.8 %all-gather.3.cloned.1.call-done = bf16[1024,576]{0,1:T(8,128)(2,1)} async-done(((bf16[128,576]{0,1:T(8,128)(2,1)}), bf16[1024,576]{0,1:T(8,128)(2,1)}) %all-gather.3.cloned.1.call-update) | async-done | bytes 1179664 | tf_op jit(solution)/shard_map/all_gather | solution.py:69
  36.1 6.8 %fusion.5 = (f32[2048]{0:T(1024)S(1)}, f32[2048,1024]{0,1:T(8,128)S(1)}) fusion(s32[2048]{0:T(1024)S(1)} %get-tuple-element.7, s32[2048]{0:T(1024)S(1)} %get-tuple-element.8, s32[1024]{0:T(1024)S(1)} %convert_reduce_fusion, bf16[2048,576]{1,0:T(8,128)(2,1)} %bitcast.93, bf16[1024,576]{0,1:T(8,128)(2,1)} %all-gather.3.cloned.1.call-done), kind=kOutput, calls=%fused_computation.13 | convolution fusion | flops 2428499968 | bytes 11956224 | tf_op jit(solution)/shard_map/dot_general | solution.py:74
  43.0 0.0 slice-start
  43.0 3.6 fusion.7
  46.6 0.0 copy-start.4
  46.6 0.0 slice-start.1
  46.7 0.0 slice-start.2
  46.7 0.0 slice-start.3
  46.7 3.8 divide_convert_fusion
  50.5 0.8 convolution_convert_fusion.2
  51.3 0.7 slice-done.3
  52.0 3.4 fusion.6
  55.3 0.0 reduce-scatter.3.cloned.1.call-update
  55.4 0.0 all-gather.5.cloned.1.call-start
  55.4 0.1 copy.38
  55.5 0.1 eq.48
  55.6 0.1 eq.44
  55.7 4.5 reduce-window.19
  60.2 0.1 slice.35
  60.3 0.1 copy.40
  60.5 0.1 copy.41
  60.6 0.1 copy.37
  60.7 0.1 mul.68
  60.8 0.1 broadcast_add_fusion
  60.9 4.3 scatter_custom_fusion.1
  65.3 4.6 scatter_custom_fusion
  69.8 0.1 broadcast_in_dim.53
  69.9 12.8 %reduce-scatter.3.cloned.1.call-done = bf16[1024,128]{0,1:T(8,128)(2,1)} async-done(((bf16[4096,128]{0,1:T(8,128)(2,1)}), bf16[1024,128]{0,1:T(8,128)(2,1)}) %reduce-scatter.3.cloned.1.call-update) | async-done | bytes 262160 | tf_op jit(solution)/shard_map/reduce_scatter | solution.py:90
  82.7 1.1 multiply_reduce_fusion
  83.8 9.4 %psum.7 = f32[128]{0:T(128)S(1)} all-reduce(f32[128]{0:T(128)S(1)} %multiply_reduce_fusion), channel_id=1, replica_groups=mesh['ctx'=8,'exp'=4] {'exp'}, use_global_device_ids=true, to_apply=%region_11.12 | all-reduce | flops 128 | bytes 1024 | tf_op jit(solution)/shard_map/psum | solution.py:99
  93.2 1.1 multiply_convert_fusion
  94.3 5.8 gather_fusion
  100.1 2.1 broadcast_select_fusion
  102.2 41.4 %all_to_all.10 = bf16[8,192,1024]{2,1,0:T(8,128)(2,1)} all-to-all(bf16[8,192,1024]{2,1,0:T(8,128)(2,1)S(1)} %broadcast_select_fusion), channel_id=1, replica_groups=mesh['ctx'=8,'exp'=4] {'ctx'}, dimensions={0} | all-to-all | bytes 6291456 | tf_op jit(solution)/shard_map/all_to_all | solution.py:122
  143.6 0.0 all-gather.5.cloned.1.call-update
  143.7 0.0 reduce-scatter.5.cloned.1.call-start
  143.7 215.0 %all-gather.5.cloned.1.call-done = bf16[8,192,4096]{2,1,0:T(8,128)(2,1)} async-done(((bf16[8,192,1024]{2,1,0:T(8,128)(2,1)}), bf16[8,192,4096]{2,1,0:T(8,128)(2,1)}) %all-gather.5.cloned.1.call-update) | async-done | bytes 12582928 | tf_op jit(solution)/shard_map/all_gather | solution.py:123
  358.8 20.5 %fusion.14 = f32[8,2,96,2,512]{4,2,3,0,1:T(8,128)} fusion(bf16[2,4096,2,512,1]{3,2,1,0,4:T(2,128)(2,1)} %bitcast.104, bf16[8,2,96,4096,1]{3,2,1,0,4:T(8,128)(2,1)} %bitcast.105), kind=kOutput, calls=%fused_computation.28 | convolution fusion | flops 12884901888 | bytes 35651584 | tf_op jit(solution)/shard_map/secd,edgf->secgf/dot_general | solution.py:26
  379.3 14.1 %convert_bitcast_fusion = bf16[8,2,96,4096]{3,2,0,1:T(8,128)(2,1)} fusion(bf16[2,512,4096]{2,1,0:T(8,128)(2,1)} %param.20, f32[8,2,96,2,512]{4,2,3,0,1:T(8,128)} %fusion.14), kind=kOutput, calls=%fused_computation.7 | convolution fusion | flops 6453460992 | bytes 27262976 | tf_op jit(solution)/shard_map/secf,efd->secd/dot_general | solution.py:30
  393.3 10.6 %copy.45 = bf16[8,2,96,4096]{3,2,1,0:T(8,128)(2,1)} copy(bf16[8,2,96,4096]{3,2,0,1:T(8,128)(2,1)} %convert_bitcast_fusion) | data formatting | bytes 25165824 | tf_op jit(solution)/shard_map/convert_element_type | solution.py:32
  403.9 0.0 reduce-scatter.5.cloned.1.call-update
  404.0 0.0 copy-start.7
  404.0 210.2 %reduce-scatter.5.cloned.1.call-done = bf16[8,192,1024]{2,1,0:T(8,128)(2,1)} async-done(((bf16[8,192,4096]{2,1,0:T(8,128)(2,1)}), bf16[8,192,1024]{2,1,0:T(8,128)(2,1)}) %reduce-scatter.5.cloned.1.call-update) | async-done | bytes 3145744 | tf_op jit(solution)/shard_map/reduce_scatter | solution.py:125
  614.2 4.5 all-to-all-start.1
  618.6 0.0 copy-done.7
  618.7 0.1 copy.46
  618.8 37.8 %all-to-all-done.1 = bf16[8,192,1024]{2,1,0:T(8,128)(2,1)} async-done(((bf16[8,192,1024]{2,1,0:T(8,128)(2,1)}), bf16[8,192,1024]{2,1,0:T(8,128)(2,1)}, u32[]{:S(2)}, u32[]{:S(2)}) %all-to-all-start.1) | async-done | bytes 3145760 | tf_op jit(solution)/shard_map/all_to_all | solution.py:127
  656.5 5.3 bitcast_convert_fusion
  661.8 9.4 %gather_fusion.1 = f32[1024,1024]{1,0:T(8,128)} fusion(f32[1536,1024]{1,0:T(8,128)} %bitcast_convert_fusion, s32[1024]{0:T(1024)S(1)} %broadcast_clamp_fusion), kind=kCustom, calls=%fused_computation.1 | custom fusion | bytes 8392704 | tf_op jit(solution)/shard_map/gather | solution.py:131
  671.2 3.5 fusion.9
  674.7 0.8 add_convert_fusion
  (32 shorter events, 0.2 us)
Async XLA Ops:
  6.5 5.3 copy-start
  6.5 29.6 %all-gather.3.cloned.1.call-start = ((), (), s32[]{:S(2)}) async-start(), calls=%async_computation.4 | async-start | bytes 1327104 | tf_op jit(solution)/shard_map/all_gather | solution.py:69
  7.3 75.4 %reduce-scatter.3.cloned.1.call-start = ((), (), s32[]{:S(2)}) async-start(), calls=%async_computation.5 | async-start | bytes 1310720 | tf_op jit(solution)/shard_map/reduce_scatter | solution.py:90
  43.0 3.7 copy-start.8
  43.0 8.3 %slice-start = ((s8[16777216]{0:T(1024)(128)(4,1)}), s8[4194304]{0:T(1024)(128)(4,1)S(1)}, s32[]{:S(2)}) async-start(s8[16777216]{0:T(1024)(128)(4,1)} %bitcast.87), calls=%async_computation.8 | async-start | bytes 8388608
  46.6 3.8 copy-start.4
  46.6 4.6 slice-start.1
  46.7 4.6 slice-start.2
  46.7 5.3 slice-start.3
  51.9 3.5 copy-start.5
  51.9 30.7 %copy-start.2 = (bf16[128,1024]{1,0:T(8,128)(2,1)S(1)}, bf16[128,1024]{1,0:T(8,128)(2,1)}, u32[]{:S(2)}) copy-start(bf16[128,1024]{1,0:T(8,128)(2,1)} %param.17) | copy-start | bytes 786436
  52.0 41.3 %copy-start.6 = (f32[1024]{0:T(1024)S(1)}, f32[1024]{0:T(1024)}, u32[]{:S(2)}) copy-start(f32[1024]{0:T(1024)} %param.18) | copy-start | bytes 12292
  55.4 303.4 %all-gather.5.cloned.1.call-start = ((), (), s32[]{:S(2)}) async-start(), calls=%async_computation.6 | async-start | bytes 15728640 | tf_op jit(solution)/shard_map/all_gather | solution.py:123
  143.7 470.5 %reduce-scatter.5.cloned.1.call-start = ((), (), s32[]{:S(2)}) async-start(), calls=%async_computation.7 | async-start | bytes 15728640 | tf_op jit(solution)/shard_map/reduce_scatter | solution.py:125
  404.0 214.7 %copy-start.7 = (f32[128,8]{0,1:T(8,128)S(1)}, f32[128,8]{0,1:T(8,128)}, u32[]{:S(2)}) copy-start(f32[128,8]{0,1:T(8,128)} %param.22) | copy-start | bytes 12292
  614.2 42.4 %all-to-all-start.1 = ((bf16[8,192,1024]{2,1,0:T(8,128)(2,1)}), bf16[8,192,1024]{2,1,0:T(8,128)(2,1)}, u32[]{:S(2)}, u32[]{:S(2)}) async-start(bf16[8,192,1024]{2,1,0:T(8,128)(2,1)} %reduce-scatter.5.cloned.1.call-done), calls=%async_computation.3 | async-start | bytes 6291456 | tf_op jit(solution)/shard_map/all_to_all | solution.py:127
  661.8 13.7 %copy-start.1 = (bf16[16,512,128]{2,1,0:T(8,128)(2,1)S(1)}, bf16[16,512,128]{2,1,0:T(8,128)(2,1)}, u32[]{:S(2)}) copy-start(bf16[16,512,128]{2,1,0:T(8,128)(2,1)} %param.14) | copy-start | bytes 6291460
  671.2 3.5 copy-start.3
Sparse Core Ops, SparseCore 0:
  9.2 26.8 all-gather.2
  55.5 27.1 reduce-scatter.2
  143.8 214.9 all-gather.4
  404.1 210.0 reduce-scatter.4
where the time goes:
time: 683 us; the launch traced here: 682 us
  waiting for transfers between devices  498 us (73%)
  blocking collectives  50.8 us (7%)
  matrix products  50.1 us (7%)
  local copies, waits for them, and re-layouts  39.9 us (6%)
  other arithmetic  25 us (4%)
  between operations  13.4 us (2%)
    all_gather x1, waiting for transfers between devices, body(): rows_full = lax.all_gather(arrived, 'exp', axis=2, tiled=True)  215 us
    reduce_scatter x1, waiting for transfers between devices, body(): lax.psum_scatter(partials, 'exp', scatter_dimension=2, tiled=True)  210 us
    all_to_all x1, blocking collectives, body(): lax.all_to_all(outgoing, 'ctx', split_axis=0, concat_axis=0, tiled=True)  41.4 us
    all_to_all x1, waiting for transfers between devices, body(): lax.all_to_all(summed.astype(jnp.bfloat16), 'ctx', split_axis=0, concat_a...  37.8 us
    all_gather x1, waiting for transfers between devices, body(): piece = lax.all_gather(latent, 'ctx', axis=0, tiled=True)  21.8 us
    dot_general x1, matrix products, expert_mlp(): jnp.einsum('secd,edgf->secgf', grouped, w_in, preferred_element_type=jnp....  20.5 us
    dot_general x1, matrix products, expert_mlp(): jnp.einsum('secf,efd->secd', activated, w_out, preferred_element_type=jnp...  14.1 us
  transfers between devices with their start and end apart: 5, of which 5 were waited for; matrix products, arithmetic and copies ran while one was open for 3% of the time, Pallas kernels for 0%

commit v1 on v0

--- a/solution.py
+++ b/solution.py
@@ -20,17 +20,21 @@
     return jnp.sum((positions[:, None] >= doc_ends[None, :]).astype(jnp.int32), axis=1)
 
 
-def expert_mlp(arrived, w_in, w_out, local_experts, capacity):
-    sources = arrived.shape[0]
-    grouped = arrived.reshape(sources, local_experts, capacity, arrived.shape[2])
-    hidden_pre = jnp.einsum("secd,edgf->secgf", grouped, w_in, preferred_element_type=jnp.float32)
-    activated = (jax.nn.silu(hidden_pre[:, :, :, 0, :]) * hidden_pre[:, :, :, 1, :]).astype(
-        jnp.bfloat16
-    )
-    partials = jnp.einsum(
-        "secf,efd->secd", activated, w_out, preferred_element_type=jnp.float32
+def expert_gates(routes, gate_weights, first_expert, local_experts):
+    named = first_expert + jnp.arange(local_experts, dtype=jnp.int32)
+    hit = routes[:, :, None] == named[None, None, :]
+    return jnp.sum(jnp.where(hit, gate_weights[:, :, None], 0.0), axis=1)
+
+
+def expert_mlp(rows, inverse, gates, w_in, w_out):
+    experts, _, _, units = w_in.shape
+    hidden_pre = jnp.einsum("td,edgf->tegf", rows, w_in, preferred_element_type=jnp.float32)
+    hidden_pre = hidden_pre * inverse[:, None, None, None]
+    activated = jax.nn.silu(hidden_pre[:, :, 0, :]) * hidden_pre[:, :, 1, :] * gates[:, :, None]
+    activated = activated.astype(jnp.bfloat16).reshape(rows.shape[0], experts * units)
+    return jnp.dot(
+        activated, w_out.reshape(experts * units, w_out.shape[2]), preferred_element_type=jnp.float32
     ).astype(jnp.bfloat16)
-    return partials.reshape(sources, local_experts * capacity, w_out.shape[2])
 
 
 def body(
@@ -47,7 +51,6 @@
     gate_weights,
     doc_lengths,
 ):
-    count_ctx = lax.axis_size("ctx")
     tokens = latent.shape[0]
     heads = w_uk.shape[0]
     qk_width = NOPE + ROPE
@@ -67,6 +70,8 @@
     row_doc = jnp.tile(q_doc, heads)
     row_count = heads * tokens
     piece = lax.all_gather(latent, "ctx", axis=0, tiled=True)
+    all_routes = lax.all_gather(routes, "ctx", axis=0, tiled=True)
+    all_gates = lax.all_gather(gate_weights, "ctx", axis=0, tiled=True)
     key_pos = jnp.arange(piece.shape[0], dtype=jnp.int32)
     key_doc = document(key_pos, doc_ends)
     allowed = (row_doc[:, None] == key_doc[None, :]) & (row_pos[:, None] >= key_pos[None, :])
@@ -97,40 +102,17 @@
     ).astype(jnp.float32)
     hidden = residual.astype(jnp.float32) + attn_t.T
     squares = lax.psum(jnp.sum(hidden * hidden, axis=1), "exp")
-    normed = (hidden * lax.rsqrt(squares[:, None] / D + epsilon) * norm_gain[None, :]).astype(
-        jnp.bfloat16
-    )
+    inverse = lax.all_gather(lax.rsqrt(squares / D + epsilon), "ctx", axis=0, tiled=True)
     local_experts = w_in.shape[0]
-    experts = local_experts * count_ctx
-    capacity = tokens * TOP * 3 // (2 * experts)
-    flat_routes = routes.reshape(-1)
-    onehot = (flat_routes[:, None] == jnp.arange(experts, dtype=jnp.int32)[None, :]).astype(
-        jnp.int32
-    )
-    slot_rank = jnp.sum((jnp.cumsum(onehot, axis=0) - onehot) * onehot, axis=1)
-    slot_index = flat_routes * capacity + slot_rank
-    owner_row = (
-        jnp.zeros((experts * capacity,), jnp.int32)
-        .at[slot_index]
-        .set(jnp.arange(tokens * TOP, dtype=jnp.int32) // TOP)
-    )
-    filled = jnp.zeros((experts * capacity,), jnp.bool_).at[slot_index].set(True)
-    gate_flat = gate_weights.reshape(-1)
-    outgoing = jnp.where(filled[:, None], normed[owner_row], jnp.zeros((), jnp.bfloat16)).reshape(
-        count_ctx, local_experts * capacity, local_width
-    )
-    arrived = lax.all_to_all(outgoing, "ctx", split_axis=0, concat_axis=0, tiled=True)
-    rows_full = lax.all_gather(arrived, "exp", axis=2, tiled=True)
-    partials = expert_mlp(rows_full, w_in, w_out, local_experts, capacity)
-    summed = lax.psum_scatter(partials, "exp", scatter_dimension=2, tiled=True).astype(jnp.float32)
-    returned = (
-        lax.all_to_all(summed.astype(jnp.bfloat16), "ctx", split_axis=0, concat_axis=0, tiled=True)
-        .astype(summed.dtype)
-        .reshape(experts * capacity, local_width)
-    )
-    picked = returned[slot_index] * gate_flat[:, None]
-    moe_out = jnp.sum(picked.reshape(tokens, TOP, local_width), axis=1)
-    return (hidden + moe_out).astype(jnp.bfloat16)
+    first_expert = lax.axis_index("ctx") * local_experts
+    scaled = (hidden * norm_gain[None, :]).astype(jnp.bfloat16)
+    rows = lax.all_gather(scaled, "exp", axis=1, tiled=True)
+    rows = lax.all_gather(rows, "ctx", axis=0, tiled=True)
+    gates = expert_gates(all_routes, all_gates, first_expert, local_experts)
+    mixed = expert_mlp(rows, inverse, gates, w_in, w_out)
+    mixed = lax.psum_scatter(mixed, "ctx", scatter_dimension=0, tiled=True)
+    mixed = lax.psum_scatter(mixed, "exp", scatter_dimension=1, tiled=True)
+    return (hidden + mixed.astype(jnp.float32)).astype(jnp.bfloat16)
 
 
 def solution(mesh):

time: 683 us -> 314 us (0.46)
  waiting for transfers between devices: 498 us -> 198 us
  local copies, waits for them, and re-layouts: 39.9 us -> 4.18 us
  other arithmetic: 25 us -> 8.58 us
  blocking collectives: 50.8 us -> 36.1 us
    all_gather x1 -> x2, waiting for transfers between devices: 215 us -> 46.2 us  [the longest x1 26.7 us: body(): rows = lax.all_gather(scaled, 'exp', axis=1, tiled=True)]
    reduce_scatter x1 -> x2, waiting for transfers between devices: 210 us -> 101 us  [the longest x1 71.4 us: body(): mixed = lax.psum_scatter(mixed, 'ctx', scatter_dimension=0, tiled=True)]
    all_to_all x1 -> x0, blocking collectives: 41.4 us -> none  [body(): lax.all_to_all(outgoing, 'ctx', split_axis=0, concat_axis=0, tiled=True)]
    all_to_all x1 -> x0, waiting for transfers between devices: 37.8 us -> none  [body(): lax.all_to_all(summed.astype(jnp.bfloat16), 'ctx', split_axis=0, concat_a...]
    all_gather x0 -> x3, blocking collectives: none -> 25.9 us  [the longest x1 9.04 us: body(): all_routes = lax.all_gather(routes, 'ctx', axis=0, tiled=True)]
    gather x2 -> x0, local copies, waits for them, and re-layouts: 15.2 us -> none  [the longest x1 9.39 us: body(): picked = returned[slot_index] * gate_flat[:, None]]
    reduce_scatter x1, waiting for transfers between devices: 12.8 us -> 27.2 us  [body(): lax.psum_scatter(lax.dot_general(w_o, head_out, (((0,), (1,)), ((), ())),...]
    convert_element_type x1 -> x0, local copies, waits for them, and re-layouts: 10.6 us -> none  [expert_mlp(): partials = jnp.einsum('secf,efd->secd', activated, w_out, preferred_eleme...]
  transfers between devices with their start and end apart: 5 -> 6, of which waited for: 5 -> 6; matrix products, arithmetic and copies ran while one was open for 3% -> 2% of each run, Pallas kernels for 0% -> 0%
where the time goes in v1:
time: 314 us
  waiting for transfers between devices  198 us (63%)
  matrix products  52.7 us (17%)
  blocking collectives  36.1 us (11%)
  between operations  13.7 us (4%)
  other arithmetic  8.58 us (3%)
  local copies, waits for them, and re-layouts  4.18 us (1%)
    reduce_scatter x1, waiting for transfers between devices, body(): mixed = lax.psum_scatter(mixed, 'ctx', scatter_dimension=0, tiled=True)  71.4 us
    reduce_scatter x1, waiting for transfers between devices, body(): mixed = lax.psum_scatter(mixed, 'exp', scatter_dimension=1, tiled=True)  29.3 us
    reduce_scatter x1, waiting for transfers between devices, body(): lax.psum_scatter(lax.dot_general(w_o, head_out, (((0,), (1,)), ((), ())),...  27.2 us
    all_gather x1, waiting for transfers between devices, body(): rows = lax.all_gather(scaled, 'exp', axis=1, tiled=True)  26.7 us
    all_gather x1, waiting for transfers between devices, body(): piece = lax.all_gather(latent, 'ctx', axis=0, tiled=True)  23.3 us
    dot_general x1, matrix products, expert_mlp(): jnp.einsum('td,edgf->tegf', rows, w_in, preferred_element_type=jnp.float32)  22.9 us
    all_gather x1, waiting for transfers between devices, body(): rows = lax.all_gather(rows, 'ctx', axis=0, tiled=True)  19.6 us
    dot_general x1, matrix products, expert_mlp(): jnp.dot(activated, w_out.reshape(experts * units, w_out.shape[2]), prefer...  15.1 us
  transfers between devices with their start and end apart: 6, of which 6 were waited for; matrix products, arithmetic and copies ran while one was open for 2% of the time, Pallas kernels for 0%

profile of v1, /device:TPU:0, one launch (start us, length us, event | category | flops | bytes accessed | tf_op | source)
XLA Modules:
  0.0 313.7 jit_solution(18016201065759643836)
XLA Ops:
  6.5 0.0 copy-start
  6.5 0.0 all-gather.5.cloned.1.call-start
  6.5 0.7 all-gather.5.cloned.1.call-update
  7.3 0.0 reduce-scatter.4.cloned.1.call-start
  7.3 1.5 copy.34
  8.8 0.7 slice.21
  9.5 1.2 copy.43
  10.8 0.8 reduce-window.8
  11.6 0.1 convert_reduce_fusion
  11.7 0.1 convert_reduce_fusion.1
  11.8 0.0 copy-done
  11.8 0.8 convolution_convert_fusion.1
  12.6 0.3 pad_maximum_fusion
  12.9 23.3 %all-gather.5.cloned.1.call-done = bf16[1024,576]{0,1:T(8,128)(2,1)} async-done(((bf16[128,576]{0,1:T(8,128)(2,1)}), bf16[1024,576]{0,1:T(8,128)(2,1)}) %all-gather.5.cloned.1.call-update) | async-done | bytes 1179664 | tf_op jit(solution)/shard_map/all_gather | solution.py:72
  36.1 6.1 %fusion.4 = (f32[2048]{0:T(1024)S(1)}, f32[2048,1024]{0,1:T(8,128)S(1)}) fusion(s32[2048]{0:T(1024)S(1)} %get-tuple-element.9, s32[2048]{0:T(1024)S(1)} %get-tuple-element.10, s32[1024]{0:T(1024)S(1)} %convert_reduce_fusion, bf16[2048,576]{1,0:T(8,128)(2,1)S(1)} %bitcast.64, bf16[1024,576]{0,1:T(8,128)(2,1)} %all-gather.5.cloned.1.call-done), kind=kOutput, calls=%fused_computation.8 | convolution fusion | flops 2428499968 | bytes 11956224 | tf_op jit(solution)/shard_map/dot_general | solution.py:79
  42.2 0.0 copy-start.8
  42.2 0.0 slice-start
  42.2 3.6 %fusion.6 = f32[2048]{0:T(1024)S(1)} fusion(f32[2048,1024]{0,1:T(8,128)S(1)} %get-tuple-element.8, f32[2048]{0:T(1024)S(1)} %broadcast_maximum_fusion, s32[2048]{0:T(1024)S(1)} %get-tuple-element.9, s32[2048]{0:T(1024)S(1)} %get-tuple-element.10, s32[1024]{0:T(1024)S(1)} %convert_reduce_fusion), kind=kLoop, calls=%fused_computation.11 | loop fusion | flops 16775168 | bytes 8425472 | tf_op jit(solution)/shard_map/reduce_sum | solution.py:83
  45.9 0.0 copy-done.8
  45.9 0.0 copy-start.2
  45.9 0.0 slice-start.1
  45.9 0.0 slice-start.2
  45.9 0.0 slice-start.3
  45.9 3.8 %divide_convert_fusion = bf16[2048,512]{1,0:T(8,128)(2,1)S(1)} fusion(f32[2048]{0:T(1024)S(1)} %fusion.6, f32[2048,1024]{0,1:T(8,128)S(1)} %get-tuple-element.8, f32[2048]{0:T(1024)S(1)} %broadcast_maximum_fusion, s32[2048]{0:T(1024)S(1)} %get-tuple-element.9, s32[2048]{0:T(1024)S(1)} %get-tuple-element.10, s32[1024]{0:T(1024)S(1)} %convert_reduce_fusion, ...), kind=kOutput, calls=%fused_computation.19 | convolution fusion | flops 2166358016 | bytes 11571200 | tf_op jit(solution)/shard_map/dot_general | solution.py:84
  49.7 0.0 copy-done.2
  49.7 0.8 convolution_convert_fusion.2
  50.5 0.0 slice-done
  50.5 0.0 slice-done.1
  50.5 0.0 slice-done.2
  50.5 0.7 slice-done.3
  51.2 0.0 copy-start.5
  51.2 0.0 copy-start.6
  51.2 0.0 copy-start.7
  51.2 3.3 %fusion.5 = bf16[4096,128]{0,1:T(8,128)(2,1)} fusion(bf16[128,2048]{0,1:T(8,128)(2,1)S(1)} %bitcast.63, bf16[2048,4096]{1,0:T(8,128)(2,1)S(1)} %bitcast.60), kind=kOutput, calls=%fused_computation.10 | convolution fusion | flops 2148007936 | bytes 18350080 | tf_op jit(solution)/shard_map/dot_general | solution.py:96
  54.5 0.0 reduce-scatter.4.cloned.1.call-update
  54.6 0.0 all-gather.7.cloned.1.call-start
  54.6 27.2 %reduce-scatter.4.cloned.1.call-done = bf16[1024,128]{0,1:T(8,128)(2,1)} async-done(((bf16[4096,128]{0,1:T(8,128)(2,1)}), bf16[1024,128]{0,1:T(8,128)(2,1)}) %reduce-scatter.4.cloned.1.call-update) | async-done | bytes 262160 | tf_op jit(solution)/shard_map/reduce_scatter | solution.py:95
  81.9 0.0 copy-done.3
  81.9 0.0 copy-done.5
  81.9 1.8 multiply_convert_fusion
  83.6 0.0 all-gather.7.cloned.1.call-update
  83.7 0.0 all-gather.9.cloned.1.call-start
  83.7 26.7 %all-gather.7.cloned.1.call-done = bf16[128,4096]{1,0:T(8,128)(2,1)} async-done(((bf16[128,1024]{1,0:T(8,128)(2,1)}), bf16[128,4096]{1,0:T(8,128)(2,1)}) %all-gather.7.cloned.1.call-update) | async-done | bytes 1048592 | tf_op jit(solution)/shard_map/all_gather | solution.py:109
  110.4 0.0 all-gather.9.cloned.1.call-update
  110.4 0.0 reduce-scatter.6.cloned.1.call-start
  110.5 0.0 copy-done.6
  110.5 9.0 %all_gather.22 = s32[1024,8]{0,1:T(8,128)S(1)} all-gather(s32[128,8]{0,1:T(8,128)S(1)} %copy-done.6), channel_id=1, replica_groups=mesh['ctx'=8,'exp'=4] {'ctx'}, dimensions={0}, use_global_device_ids=true | all-gather | bytes 36864 | tf_op jit(solution)/shard_map/all_gather | solution.py:73
  119.5 0.0 copy-done.7
  119.5 9.0 %all_gather.23 = f32[1024,8]{0,1:T(8,128)S(1)} all-gather(f32[128,8]{0,1:T(8,128)S(1)} %copy-done.7), channel_id=1, replica_groups=mesh['ctx'=8,'exp'=4] {'ctx'}, dimensions={0}, use_global_device_ids=true | all-gather | bytes 36864 | tf_op jit(solution)/shard_map/all_gather | solution.py:74
  128.5 0.1 select_reduce_fusion
  128.6 10.3 %psum.7 = f32[128]{0:T(128)S(1)} all-reduce(f32[128]{0:T(128)S(1)} %get-tuple-element.6), channel_id=1, replica_groups=mesh['ctx'=8,'exp'=4] {'exp'}, use_global_device_ids=true, to_apply=%region_7.8 | all-reduce | flops 128 | bytes 1024 | tf_op jit(solution)/shard_map/psum | solution.py:104
  138.9 7.8 %all-gather = f32[8,1,128]{2,1,0:T(1,128)S(1)} all-gather(f32[1,1,128]{2,1,0:T(1,128)S(1)} %rsqrt_bitcast_fusion), channel_id=1, replica_groups=mesh['ctx'=8,'exp'=4] {'ctx'}, dimensions={0}, use_global_device_ids=true | all-gather | bytes 4608 | tf_op jit(solution)/shard_map/all_gather | solution.py:105
  146.7 19.6 %all-gather.9.cloned.1.call-done = bf16[1024,4096]{1,0:T(8,128)(2,1)} async-done(((bf16[128,4096]{1,0:T(8,128)(2,1)}), bf16[1024,4096]{1,0:T(8,128)(2,1)}) %all-gather.9.cloned.1.call-update) | async-done | bytes 8388624 | tf_op jit(solution)/shard_map/all_gather | solution.py:110
  166.3 22.9 %broadcast_multiply_fusion = f32[1024,2,2,512]{3,0,2,1:T(8,128)S(1)} fusion(f32[1024]{0:T(1024)S(1)} %bitcast.67, bf16[2,4096,2,512]{3,2,1,0:T(2,128)(2,1)} %param.19, bf16[1024,4096]{1,0:T(8,128)(2,1)} %all-gather.9.cloned.1.call-done), kind=kOutput, calls=%fused_computation.18 | convolution fusion | flops 17181966336 | bytes 33558528 | tf_op jit(solution)/shard_map/td,edgf->tegf/dot_general | solution.py:31
  189.1 0.0 copy-start.1
  189.2 15.1 %bitcast_convert_fusion = bf16[1024,4096]{1,0:T(8,128)(2,1)} fusion(bf16[2,512,4096]{2,1,0:T(8,128)(2,1)} %param.20, f32[1024,2,2,512]{3,0,2,1:T(8,128)S(1)} %broadcast_multiply_fusion, f32[1024,2]{0,1:T(2,128)S(1)} %select_reduce_fusion), kind=kOutput, calls=%fused_computation | convolution fusion | flops 8601468928 | bytes 25174016 | tf_op jit(solution)/shard_map/dot_general | solution.py:35
  204.3 0.0 reduce-scatter.6.cloned.1.call-update
  204.3 0.0 reduce-scatter.8.cloned.1.call-start
  204.4 71.4 %reduce-scatter.6.cloned.1.call-done = bf16[128,4096]{1,0:T(8,128)(2,1)} async-done(((bf16[1024,4096]{1,0:T(8,128)(2,1)}), bf16[128,4096]{1,0:T(8,128)(2,1)}) %reduce-scatter.6.cloned.1.call-update) | async-done | bytes 1048592 | tf_op jit(solution)/shard_map/reduce_scatter | solution.py:113
  275.8 0.0 reduce-scatter.8.cloned.1.call-update
  275.8 29.3 %reduce-scatter.8.cloned.1.call-done = bf16[128,1024]{1,0:T(8,128)(2,1)} async-done(((bf16[128,4096]{1,0:T(8,128)(2,1)}), bf16[128,1024]{1,0:T(8,128)(2,1)}) %reduce-scatter.8.cloned.1.call-update) | async-done | bytes 262160 | tf_op jit(solution)/shard_map/reduce_scatter | solution.py:114
  305.1 0.0 copy-done.4
  305.1 1.8 add_convert_fusion
  306.9 0.0 copy-done.1
  (8 shorter events, 0.0 us)
Async XLA Ops:
  6.5 5.3 %copy-start = (bf16[16,512,128]{2,1,0:T(8,128)(2,1)S(1)}, bf16[16,512,128]{2,1,0:T(8,128)(2,1)}, u32[]{:S(2)}) copy-start(bf16[16,512,128]{2,1,0:T(8,128)(2,1)} %param.14) | copy-start | bytes 6291460
  6.5 29.6 %all-gather.5.cloned.1.call-start = ((), (), s32[]{:S(2)}) async-start(), calls=%async_computation.3 | async-start | bytes 1327104 | tf_op jit(solution)/shard_map/all_gather | solution.py:72
  7.3 74.6 %reduce-scatter.4.cloned.1.call-start = ((), (), s32[]{:S(2)}) async-start(), calls=%async_computation.4 | async-start | bytes 1310720 | tf_op jit(solution)/shard_map/reduce_scatter | solution.py:95
  42.2 3.7 %copy-start.8 = (bf16[1024,576]{0,1:T(8,128)(2,1)S(1)}, bf16[1024,576]{0,1:T(8,128)(2,1)}, u32[]{:S(2)}) copy-start(bf16[1024,576]{0,1:T(8,128)(2,1)} %all-gather.5.cloned.1.call-done) | copy-start | bytes 3538948
  42.2 8.3 %slice-start = ((s8[16777216]{0:T(1024)(128)(4,1)}), s8[4194304]{0:T(1024)(128)(4,1)S(1)}, s32[]{:S(2)}) async-start(s8[16777216]{0:T(1024)(128)(4,1)} %bitcast.59), calls=%async_computation.9 | async-start | bytes 8388608
  45.9 3.8 %copy-start.2 = (bf16[16,512,128]{2,1,0:T(8,128)(2,1)S(1)}, bf16[16,512,128]{2,1,0:T(8,128)(2,1)}, u32[]{:S(2)}) copy-start(bf16[16,512,128]{2,1,0:T(8,128)(2,1)} %param.15) | copy-start | bytes 6291460
  45.9 4.6 %slice-start.1 = ((s8[16777216]{0:T(1024)(128)(4,1)}), s8[4194304]{0:T(1024)(128)(4,1)S(1)}, s32[]{:S(2)}) async-start(s8[16777216]{0:T(1024)(128)(4,1)} %bitcast.59), calls=%async_computation.10 | async-start | bytes 8388608
  45.9 4.6 %slice-start.2 = ((s8[16777216]{0:T(1024)(128)(4,1)}), s8[4194304]{0:T(1024)(128)(4,1)S(1)}, s32[]{:S(2)}) async-start(s8[16777216]{0:T(1024)(128)(4,1)} %bitcast.59), calls=%async_computation.11 | async-start | bytes 8388608
  45.9 5.3 %slice-start.3 = ((s8[16777216]{0:T(1024)(128)(4,1)}), s8[4194304]{0:T(1024)(128)(4,1)S(1)}, s32[]{:S(2)}) async-start(s8[16777216]{0:T(1024)(128)(4,1)} %bitcast.59), calls=%async_computation.12 | async-start | bytes 8388608
  51.2 30.7 %copy-start.3 = (bf16[128,1024]{1,0:T(8,128)(2,1)S(1)}, bf16[128,1024]{1,0:T(8,128)(2,1)}, u32[]{:S(2)}) copy-start(bf16[128,1024]{1,0:T(8,128)(2,1)} %param.17) | copy-start | bytes 786436
  51.2 30.7 %copy-start.5 = (f32[1024]{0:T(1024)S(1)}, f32[1024]{0:T(1024)}, u32[]{:S(2)}) copy-start(f32[1024]{0:T(1024)} %param.18) | copy-start | bytes 12292
  51.2 59.3 %copy-start.6 = (s32[128,8]{0,1:T(8,128)S(1)}, s32[128,8]{0,1:T(8,128)}, u32[]{:S(2)}) copy-start(s32[128,8]{0,1:T(8,128)} %param.21) | copy-start | bytes 12292
  51.2 68.3 %copy-start.7 = (f32[128,8]{0,1:T(8,128)S(1)}, f32[128,8]{0,1:T(8,128)}, u32[]{:S(2)}) copy-start(f32[128,8]{0,1:T(8,128)} %param.22) | copy-start | bytes 12292
  54.6 55.8 %all-gather.7.cloned.1.call-start = ((), (), s32[]{:S(2)}) async-start(), calls=%async_computation.5 | async-start | bytes 1310720 | tf_op jit(solution)/shard_map/all_gather | solution.py:109
  83.7 82.6 %all-gather.9.cloned.1.call-start = ((), (), s32[]{:S(2)}) async-start(), calls=%async_computation.6 | async-start | bytes 9437184 | tf_op jit(solution)/shard_map/all_gather | solution.py:110
  110.4 165.4 %reduce-scatter.6.cloned.1.call-start = ((), (), s32[]{:S(2)}) async-start(), calls=%async_computation.7 | async-start | bytes 9437184 | tf_op jit(solution)/shard_map/reduce_scatter | solution.py:113
  189.1 117.7 %copy-start.1 = (bf16[16,512,128]{2,1,0:T(8,128)(2,1)S(1)}, bf16[16,512,128]{2,1,0:T(8,128)(2,1)}, u32[]{:S(2)}) copy-start(bf16[16,512,128]{2,1,0:T(8,128)(2,1)} %param.14) | copy-start | bytes 6291460
  204.3 100.8 %copy-start.4 = (bf16[1024,128]{0,1:T(8,128)(2,1)S(1)}, bf16[1024,128]{0,1:T(8,128)(2,1)}, u32[]{:S(2)}) copy-start(bf16[1024,128]{0,1:T(8,128)(2,1)} %reduce-scatter.4.cloned.1.call-done) | copy-start | bytes 786436
  204.3 100.8 %reduce-scatter.8.cloned.1.call-start = ((), (), s32[]{:S(2)}) async-start(), calls=%async_computation.8 | async-start | bytes 1310720 | tf_op jit(solution)/shard_map/reduce_scatter | solution.py:114
Sparse Core Ops, SparseCore 0:
  9.2 26.8 all-gather.4
  54.7 27.1 reduce-scatter.3
  83.8 26.5 all-gather.6
  112.3 53.9 all-gather.8
  204.4 71.2 reduce-scatter.5
  277.9 27.1 reduce-scatter.7

commit v2 on v1

--- a/solution.py
+++ b/solution.py
@@ -1,8 +1,11 @@
+import functools
 import math
 
 import jax
 import jax.numpy as jnp
 from jax import lax
+from jax.experimental import pallas as pl
+from jax.experimental.pallas import tpu as pltpu
 from jax.sharding import PartitionSpec as P
 
 D = 4096
@@ -20,9 +23,347 @@
     return jnp.sum((positions[:, None] >= doc_ends[None, :]).astype(jnp.int32), axis=1)
 
 
-def expert_gates(routes, gate_weights, first_expert, local_experts):
-    named = first_expert + jnp.arange(local_experts, dtype=jnp.int32)
-    hit = routes[:, :, None] == named[None, None, :]
+MESH = pl.DeviceIdType.MESH
+
+
+def ring_place(chip, chips):
+    half = chips // 2
+    return chip + (chip // half) * (chips - 1 + half - 2 * chip)
+
+
+def ring_member(place, chips, core):
+    return ring_place(lax.rem(place + chips, chips), chips) * 2 + core
+
+
+def by_distance(count):
+    return sorted(range(count), key=lambda step: min(step, count - step))
+
+
+def greet(peers):
+    barrier = pltpu.get_barrier_semaphore()
+    for peer in peers:
+        pl.semaphore_signal(barrier, inc=1, device_id=peer, device_id_type=MESH)
+    pl.semaphore_wait(barrier, len(peers))
+
+
+def neighbours(chips, count_exp):
+    ctx, exp = lax.axis_index("ctx"), lax.axis_index("exp")
+    core = lax.rem(ctx, 2)
+    place = ring_place(ctx // 2, chips)
+    sibling = (ctx + 1 - 2 * core, exp)
+    right = (ring_member(place + 1, chips, core), exp)
+    left = (ring_member(place - 1, chips, core), exp)
+    across = [(ctx, lax.rem(exp + step, count_exp)) for step in range(count_exp)]
+    return ctx, exp, core, place, sibling, (right, left), across
+
+
+def gather_kernel(chips, count_exp, with_extra, *refs):
+    if with_extra:
+        own_ref, extra_ref, out_ref, extra_out = refs[:4]
+        refs = refs[4:]
+    else:
+        own_ref, out_ref = refs[:2]
+        extra_ref = extra_out = None
+        refs = refs[2:]
+    local_sem, z_send, z_recv, ring_send, ring_recv, sib_send, sib_recv = refs
+    ctx, exp, core, place, sibling, sides, across = neighbours(chips, count_exp)
+    half = chips // 2
+    rows, cols = own_ref.shape
+    chunks = by_distance(count_exp) + (["extra"] if with_extra else [])
+    slot_of = {chunk: at for at, chunk in enumerate(chunks)}
+    greet([*across[1:], *sides, sibling])
+
+    def block(owner, chunk, part):
+        if chunk == "extra":
+            height = extra_ref.shape[0] * count_exp
+            return extra_out.at[pl.ds(pl.multiple_of(owner * height, height), height)]
+        start, height = (0, rows) if part is None else (part * (rows // 2), rows // 2)
+        down = pl.ds(pl.multiple_of(owner * rows + start, rows // 2), height)
+        if count_exp == 1:
+            return out_ref.at[down]
+        column = lax.rem(exp - chunk + count_exp, count_exp) * cols
+        return out_ref.at[down, pl.ds(pl.multiple_of(column, cols), cols)]
+
+    def extra_block(which):
+        height = extra_ref.shape[0]
+        at = (ctx * count_exp + which) * height
+        return extra_out.at[pl.ds(pl.multiple_of(at, height), height)]
+
+    started = []
+
+    def send(source, target, sems, at, device):
+        copy = pltpu.make_async_remote_copy(
+            src_ref=source,
+            dst_ref=target,
+            send_sem=sems[0].at[at],
+            recv_sem=sems[1].at[at],
+            device_id=device,
+            device_id_type=MESH,
+        )
+        copy.start()
+        started.append(copy)
+        return copy
+
+    keeps = [pltpu.make_async_copy(own_ref, block(ctx, 0, None), local_sem.at[0])]
+    if with_extra:
+        keeps.append(pltpu.make_async_copy(extra_ref, extra_block(exp), local_sem.at[1]))
+    for keep in keeps:
+        keep.start()
+    arriving = {}
+    z_sems = (z_send, z_recv)
+    for step in range(1, count_exp):
+        if with_extra:
+            arriving["extra", step] = send(
+                extra_ref, extra_block(exp), z_sems, count_exp + step, across[step]
+            )
+    for step in by_distance(count_exp)[1:]:
+        arriving[step] = send(own_ref, block(ctx, 0, None), z_sems, step, across[step])
+    for keep in keeps:
+        keep.wait()
+
+    ring_sems, sib_sems = (ring_send, ring_recv), (sib_send, sib_recv)
+    ring, sib = {}, []
+
+    def share(owner, chunk, part, at):
+        piece = block(owner, chunk, part)
+        sib.append(send(piece, piece, sib_sems, at, sibling))
+
+    def hop_on(chunk, hop, side):
+        if chunk == "extra" and hop == half and side == 1:
+            return
+        part = side if hop == half and chunk != "extra" else None
+        source = ring_member(place - (hop - 1) * (1 - 2 * side), chips, core)
+        piece = block(source, chunk, part)
+        at = (side * half + hop - 1) * len(chunks) + slot_of[chunk]
+        ring[chunk, hop, side] = send(piece, piece, ring_sems, at, sides[side])
+
+    def arrive(chunk, hop):
+        for side in range(2):
+            if (chunk, hop, side) not in ring:
+                continue
+            ring[chunk, hop, side].wait_recv()
+            if hop < half:
+                hop_on(chunk, hop + 1, side)
+        for side in range(2):
+            if (chunk, hop, side) not in ring:
+                continue
+            part = side if hop == half and chunk != "extra" else None
+            source = ring_member(place - hop * (1 - 2 * side), chips, core)
+            at = len(chunks) + (side * half + hop - 1) * len(chunks) + slot_of[chunk]
+            share(source, chunk, part, at)
+
+    for turn in range(len(chunks) + half):
+        if turn < len(chunks):
+            chunk = chunks[turn]
+            if chunk == "extra":
+                for step in range(1, count_exp):
+                    arriving["extra", step].wait_recv()
+            elif chunk != 0:
+                arriving[chunk].wait_recv()
+            for side in range(2):
+                hop_on(chunk, 1, side)
+            share(ctx, chunk, None, slot_of[chunk])
+        for hop in range(1, half + 1):
+            if 0 <= turn - hop < len(chunks):
+                arrive(chunks[turn - hop], hop)
+    for copy in sib:
+        copy.wait_recv()
+    for copy in started:
+        copy.wait_send()
+
+
+def gather(count_ctx, count_exp, own, extra, collective_id):
+    chips = count_ctx // 2
+    half = chips // 2
+    rows, cols = own.shape
+    outs = [jax.ShapeDtypeStruct((count_ctx * rows, count_exp * cols), own.dtype)]
+    operands = [own]
+    if extra is not None:
+        operands.append(extra)
+        outs.append(
+            jax.ShapeDtypeStruct((count_ctx * count_exp * extra.shape[0], extra.shape[1]), extra.dtype)
+        )
+    chunks = count_exp + len(operands) - 1
+    dma = pltpu.SemaphoreType.DMA
+    result = pl.pallas_call(
+        functools.partial(gather_kernel, chips, count_exp, extra is not None),
+        out_shape=outs,
+        in_specs=[pl.BlockSpec(memory_space=pl.ANY)] * len(operands),
+        out_specs=[pl.BlockSpec(memory_space=pl.ANY)] * len(outs),
+        scratch_shapes=[
+            dma((2,)),
+            dma((2 * count_exp,)),
+            dma((2 * count_exp,)),
+            dma((2 * half * chunks,)),
+            dma((2 * half * chunks,)),
+            dma(((2 * half + 1) * chunks,)),
+            dma(((2 * half + 1) * chunks,)),
+        ],
+        compiler_params=pltpu.CompilerParams(collective_id=collective_id, has_side_effects=True),
+    )(*operands)
+    return result if extra is not None else result[0]
+
+
+def scatter_kernel(
+    chips, count_exp, sums_ref, out_ref, held, passed, landed, leaving, returned,
+    load_sem, sib_send, sib_recv, ring_send, ring_recv, z_send, z_recv,
+):
+    ctx, exp, core, place, sibling, sides, across = neighbours(chips, count_exp)
+    half = chips // 2
+    rows, cols = out_ref.shape
+    order = by_distance(count_exp)[::-1]
+    greet([*across[1:], *sides, sibling])
+
+    def block(owner, chunk):
+        column = across[chunk][1] * cols
+        return sums_ref.at[
+            pl.ds(pl.multiple_of(owner * rows, rows), rows),
+            pl.ds(pl.multiple_of(column, cols), cols),
+        ]
+
+    started = []
+
+    def send(source, target, sems, at, device):
+        copy = pltpu.make_async_remote_copy(
+            src_ref=source,
+            dst_ref=target,
+            send_sem=sems[0].at[at],
+            recv_sem=sems[1].at[at],
+            device_id=device,
+            device_id_type=MESH,
+        )
+        copy.start()
+        started.append(copy)
+        return copy
+
+    loads, swaps = {}, {}
+    offsets = sorted(range(chips), key=lambda offset: -min(offset, chips - offset))
+    for chunk in order:
+        for offset in offsets:
+            at = offset * count_exp + chunk
+            theirs = ring_member(place + offset, chips, 1 - core)
+            mine = ring_member(place + offset, chips, core)
+            swaps[offset, chunk] = send(
+                block(theirs, chunk), passed.at[at], (sib_send, sib_recv), at, sibling
+            )
+            loads[offset, chunk] = pltpu.make_async_copy(
+                block(mine, chunk), held.at[at], load_sem.at[at]
+            )
+            loads[offset, chunk].start()
+
+    def pair(offset, chunk):
+        loads[offset, chunk].wait()
+        swaps[offset, chunk].wait_recv()
+        at = offset * count_exp + chunk
+        return held[at].astype(jnp.float32) + passed[at].astype(jnp.float32)
+
+    ring = {}
+    stretch = rows // 2
+
+    def ring_slot(side, step, chunk):
+        return (side * half + step - 1) * count_exp + chunk
+
+    def pass_on(offset, side, step, chunk):
+        at = offset * count_exp + chunk
+        slot = ring_slot(side, step, chunk)
+        source, target = held.at[at], landed.at[slot]
+        if step == 1:
+            source = source.at[pl.ds(side * stretch, stretch)]
+            target = target.at[pl.ds(side * stretch, stretch)]
+        ring[side, step, chunk] = send(source, target, (ring_send, ring_recv), slot, sides[side])
+
+    def begin(chunk):
+        at = half * count_exp + chunk
+        held[at] = pair(half, chunk).astype(held.dtype)
+        for side in range(2):
+            pass_on(half, side, 1, chunk)
+
+    def middle(chunk, step):
+        for side in range(2):
+            offset = half - step + 1
+            offset = offset if side == 0 else chips - offset
+            at = offset * count_exp + chunk
+            held[at] = pair(offset, chunk).astype(held.dtype)
+            ring[side, step - 1, chunk].wait_recv()
+            slot = ring_slot(side, step - 1, chunk)
+            part = pl.ds(side * stretch, stretch) if step == 2 else pl.ds(0, rows)
+            held[at, part] = (
+                held[at, part].astype(jnp.float32) + landed[slot, part].astype(jnp.float32)
+            ).astype(held.dtype)
+            pass_on(offset, side, step, chunk)
+
+    back = {}
+
+    def finish(chunk):
+        total = pair(0, chunk)
+        for side in range(2):
+            ring[side, half, chunk].wait_recv()
+            total += landed[ring_slot(side, half, chunk)].astype(jnp.float32)
+        if chunk == 0:
+            out_ref[...] = total
+        else:
+            leaving[chunk] = total.astype(leaving.dtype)
+            back[chunk] = send(
+                leaving.at[chunk], returned.at[chunk], (z_send, z_recv), chunk, across[chunk]
+            )
+
+    for turn in range(count_exp + half):
+        if turn < count_exp:
+            begin(order[turn])
+        for step in range(2, half + 1):
+            if 0 <= turn - step + 1 < count_exp:
+                middle(order[turn - step + 1], step)
+        if 0 <= turn - half < count_exp:
+            finish(order[turn - half])
+    total = out_ref[...]
+    for chunk in order[:-1]:
+        back[chunk].wait_recv()
+        total += returned[chunk].astype(jnp.float32)
+    out_ref[...] = total
+    for copy in started:
+        copy.wait_send()
+
+
+def scatter(count_ctx, count_exp, sums, collective_id):
+    chips = count_ctx // 2
+    half = chips // 2
+    rows, cols = sums.shape[0] // count_ctx, sums.shape[1] // count_exp
+    dma = pltpu.SemaphoreType.DMA
+    blocks, hops = chips * count_exp, 2 * half * count_exp
+    return pl.pallas_call(
+        functools.partial(scatter_kernel, chips, count_exp),
+        out_shape=jax.ShapeDtypeStruct((rows, cols), jnp.float32),
+        in_specs=[pl.BlockSpec(memory_space=pl.ANY)],
+        out_specs=pl.BlockSpec(memory_space=pltpu.VMEM),
+        scratch_shapes=[
+            pltpu.VMEM((blocks, rows, cols), sums.dtype),
+            pltpu.VMEM((blocks, rows, cols), sums.dtype),
+            pltpu.VMEM((hops, rows, cols), sums.dtype),
+            pltpu.VMEM((count_exp, rows, cols), sums.dtype),
+            pltpu.VMEM((count_exp, rows, cols), sums.dtype),
+            dma((blocks,)),
+            dma((blocks,)),
+            dma((blocks,)),
+            dma((hops,)),
+            dma((hops,)),
+            dma((count_exp,)),
+            dma((count_exp,)),
+        ],
+        compiler_params=pltpu.CompilerParams(
+            collective_id=collective_id, has_side_effects=True, vmem_limit_bytes=40 * 1024 * 1024
+        ),
+    )(sums)
+
+
+def three_terms(values):
+    first = lax.reduce_precision(values, 8, 7)
+    second = lax.reduce_precision(values - first, 8, 7)
+    third = values - first - second
+    return [term.astype(jnp.bfloat16) for term in (first, second, third)]
+
+
+def dense_gates(routes, gate_weights, experts):
+    hit = routes[:, :, None] == jnp.arange(experts, dtype=jnp.int32)[None, None, :]
     return jnp.sum(jnp.where(hit, gate_weights[:, :, None], 0.0), axis=1)
 
 
@@ -51,6 +392,7 @@
     gate_weights,
     doc_lengths,
 ):
+    count_ctx, count_exp = lax.axis_size("ctx"), lax.axis_size("exp")
     tokens = latent.shape[0]
     heads = w_uk.shape[0]
     qk_width = NOPE + ROPE
@@ -69,9 +411,21 @@
     row_pos = jnp.tile(q_pos, heads)
     row_doc = jnp.tile(q_doc, heads)
     row_count = heads * tokens
-    piece = lax.all_gather(latent, "ctx", axis=0, tiled=True)
-    all_routes = lax.all_gather(routes, "ctx", axis=0, tiled=True)
-    all_gates = lax.all_gather(gate_weights, "ctx", axis=0, tiled=True)
+    local_experts = w_in.shape[0]
+    experts = local_experts * count_ctx
+    own_gates = three_terms(dense_gates(routes, gate_weights, experts))
+    width = LAT + ROPE
+    spare = -(width + 3 * experts) % 128
+    packed = jnp.concatenate(
+        [latent, *own_gates, jnp.zeros((tokens, spare), jnp.bfloat16)], axis=1
+    )
+    packed = gather(count_ctx, 1, packed, None, 0)
+    piece = packed[:, :width]
+    all_gates = jnp.sum(
+        packed[:, width : width + 3 * experts].astype(jnp.float32).reshape(-1, 3, experts), axis=1
+    )
+    first_expert = lax.axis_index("ctx") * local_experts
+    gates = lax.dynamic_slice_in_dim(all_gates, first_expert, local_experts, axis=1)
     key_pos = jnp.arange(piece.shape[0], dtype=jnp.int32)
     key_doc = document(key_pos, doc_ends)
     allowed = (row_doc[:, None] == key_doc[None, :]) & (row_pos[:, None] >= key_pos[None, :])
@@ -101,18 +455,15 @@
         tiled=True,
     ).astype(jnp.float32)
     hidden = residual.astype(jnp.float32) + attn_t.T
-    squares = lax.psum(jnp.sum(hidden * hidden, axis=1), "exp")
-    inverse = lax.all_gather(lax.rsqrt(squares / D + epsilon), "ctx", axis=0, tiled=True)
-    local_experts = w_in.shape[0]
-    first_expert = lax.axis_index("ctx") * local_experts
+    squares = jnp.sum(hidden * hidden, axis=1)
     scaled = (hidden * norm_gain[None, :]).astype(jnp.bfloat16)
-    rows = lax.all_gather(scaled, "exp", axis=1, tiled=True)
-    rows = lax.all_gather(rows, "ctx", axis=0, tiled=True)
-    gates = expert_gates(all_routes, all_gates, first_expert, local_experts)
-    mixed = expert_mlp(rows, inverse, gates, w_in, w_out)
-    mixed = lax.psum_scatter(mixed, "ctx", scatter_dimension=0, tiled=True)
-    mixed = lax.psum_scatter(mixed, "exp", scatter_dimension=1, tiled=True)
-    return (hidden + mixed.astype(jnp.float32)).astype(jnp.bfloat16)
+    rows, squares = gather(
+        count_ctx, count_exp, scaled, jnp.broadcast_to(squares[None, :], (8, tokens)), 1
+    )
+    squares = jnp.sum(squares.reshape(count_ctx, count_exp, 8, tokens)[:, :, 0], axis=1)
+    inverse = lax.rsqrt(squares.reshape(-1) / D + epsilon)
+    mixed = scatter(count_ctx, count_exp, expert_mlp(rows, inverse, gates, w_in, w_out), 2)
+    return (hidden + mixed).astype(jnp.bfloat16)
 
 
 def solution(mesh):

time: 314 us -> 226 us (0.72)
  waiting for transfers between devices: 198 us -> 26.3 us
  Pallas kernels: 0 us -> 113 us
  blocking collectives: 36.1 us -> 0 us
  local copies, waits for them, and re-layouts: 4.18 us -> 9.35 us
    pallas_call x0 -> x3, Pallas kernels: none -> 113 us  [the longest x2 70.5 us: gather(): pl.pallas_call(functools.partial(gather_kernel, chips, count_exp, extra i...]
    reduce_scatter x2 -> x0, waiting for transfers between devices: 101 us -> none  [the longest x1 71.4 us: body(): mixed = lax.psum_scatter(mixed, 'ctx', scatter_dimension=0, tiled=True)]
    all_gather x3 -> x0, waiting for transfers between devices: 69.5 us -> none  [the longest x1 26.7 us: body(): rows = lax.all_gather(scaled, 'exp', axis=1, tiled=True)]
    all_gather x3 -> x0, blocking collectives: 25.9 us -> none  [the longest x1 9.04 us: body(): all_routes = lax.all_gather(routes, 'ctx', axis=0, tiled=True)]
    psum x1 -> x0, blocking collectives: 10.3 us -> none  [body(): squares = lax.psum(jnp.sum(hidden * hidden, axis=1), 'exp')]
    reduce_sum x1 -> x4, other arithmetic: 0.1 us -> 3.57 us  [the longest x1 1.76 us: body(): squares = jnp.sum(hidden * hidden, axis=1)]
  transfers between devices with their start and end apart: 6 -> 1, of which waited for: 6 -> 1; matrix products, arithmetic and copies ran while one was open for 2% -> 1% of each run, Pallas kernels for 0% -> 0%
where the time goes in v2:
time: 226 us
  Pallas kernels  113 us (50%)
  matrix products  51.7 us (23%)
  waiting for transfers between devices  26.3 us (12%)
  between operations  13.7 us (6%)
  other arithmetic  11.6 us (5%)
  local copies, waits for them, and re-layouts  9.35 us (4%)
    pallas_call x2, Pallas kernels, gather(): pl.pallas_call(functools.partial(gather_kernel, chips, count_exp, extra i...  70.5 us
    pallas_call x1, Pallas kernels, scatter(): pl.pallas_call(functools.partial(scatter_kernel, chips, count_exp), out_s...  42.7 us
    reduce_scatter x1, waiting for transfers between devices, body(): lax.psum_scatter(lax.dot_general(w_o, head_out, (((0,), (1,)), ((), ())),...  26.3 us
    dot_general x1, matrix products, expert_mlp(): jnp.einsum('td,edgf->tegf', rows, w_in, preferred_element_type=jnp.float32)  24.5 us
    dot_general x1, matrix products, expert_mlp(): jnp.dot(activated, w_out.reshape(experts * units, w_out.shape[2]), prefer...  14.3 us
    unnamed x27, local copies, waits for them, and re-layouts  5.19 us
  transfers between devices with their start and end apart: 1, of which 1 were waited for; matrix products, arithmetic and copies ran while one was open for 1% of the time, Pallas kernels for 0%

profile of v2, /device:TPU:0, one launch (start us, length us, event | category | flops | bytes accessed | tf_op | source)
XLA Modules:
  0.0 225.9 jit_solution(9938244354669439913)
XLA Ops:
  6.5 0.0 copy-start
  6.5 0.0 reduce-scatter.2.cloned.1.call-start
  6.5 0.9 select_reduce_fusion
  7.4 0.1 copy.42
  7.5 0.8 reduce-window.8
  8.4 0.7 convert_reduce_fusion
  9.0 0.1 convert_reduce_fusion.1
  9.1 0.7 copy.45
  9.9 0.1 copy.43
  10.0 1.7 copy.44
  11.7 1.5 copy.39
  13.2 0.7 slice.34
  13.9 1.2 copy.53
  15.1 0.6 fusion.26
  15.8 0.0 copy-start.6
  15.8 1.7 concatenate.7.refs_0_
  17.5 20.1 %shard_map.118 = bf16[1024,640]{1,0:T(8,128)(2,1)} custom-call(bf16[128,640]{1,0:T(8,128)(2,1)} %concatenate.7.refs_0_), custom_call_target="tpu_custom_call" | custom-call | tf_op jit(solution)/shard_map/pallas_call | solution.py:188
  37.6 0.0 copy-done
  37.6 0.0 copy-start.3
  37.6 0.8 convolution_convert_fusion.1
  38.3 0.3 pad_maximum_fusion
  38.6 0.0 copy-done.6
  38.6 0.2 copy-done.3
  38.9 4.1 %fusion.4 = (f32[2048]{0:T(1024)S(1)}, f32[2048,1024]{0,1:T(8,128)S(1)}) fusion(s32[2048]{0:T(1024)S(1)} %get-tuple-element.17, s32[2048]{0:T(1024)S(1)} %get-tuple-element.18, s32[1024]{0:T(1024)S(1)} %copy-done.6, bf16[2048,576]{1,0:T(8,128)(2,1)S(1)} %bitcast.64, bf16[1024,640]{1,0:T(8,128)(2,1)S(1)} %copy-done.3), kind=kOutput, calls=%fused_computation.8 | convolution fusion | flops 2428499968 | bytes 12087296 | tf_op jit(solution)/shard_map/dot_general | solution.py:433
  43.0 0.0 slice-start
  43.0 3.6 %fusion.6 = f32[2048]{0:T(1024)S(1)} fusion(f32[2048,1024]{0,1:T(8,128)S(1)} %get-tuple-element.16, f32[2048]{0:T(1024)S(1)} %broadcast_maximum_fusion, s32[2048]{0:T(1024)S(1)} %get-tuple-element.17, s32[2048]{0:T(1024)S(1)} %get-tuple-element.18, s32[1024]{0:T(1024)S(1)} %copy-done.6), kind=kLoop, calls=%fused_computation.11 | loop fusion | flops 16775168 | bytes 8425472 | tf_op jit(solution)/shard_map/reduce_sum | solution.py:437
  46.6 0.0 copy-start.2
  46.6 0.0 slice-start.1
  46.6 0.0 slice-start.2
  46.7 0.0 slice-start.3
  46.7 4.0 %divide_convert_fusion = bf16[2048,512]{1,0:T(8,128)(2,1)S(1)} fusion(f32[2048]{0:T(1024)S(1)} %fusion.6, f32[2048,1024]{0,1:T(8,128)S(1)} %get-tuple-element.16, f32[2048]{0:T(1024)S(1)} %broadcast_maximum_fusion, s32[2048]{0:T(1024)S(1)} %get-tuple-element.17, s32[2048]{0:T(1024)S(1)} %get-tuple-element.18, s32[1024]{0:T(1024)S(1)} %copy-done.6, ...), kind=kOutput, calls=%fused_computation.19 | convolution fusion | flops 2166358016 | bytes 11571200 | tf_op jit(solution)/shard_map/dot_general | solution.py:438
  50.6 0.0 copy-done.2
  50.7 0.8 convolution_convert_fusion.2
  51.4 0.0 slice-done
  51.4 0.0 slice-done.1
  51.4 0.0 slice-done.2
  51.5 0.5 slice-done.3
  51.9 0.0 copy-start.4
  51.9 0.0 copy-start.7
  51.9 3.4 %fusion.5 = bf16[4096,128]{0,1:T(8,128)(2,1)} fusion(bf16[128,2048]{0,1:T(8,128)(2,1)S(1)} %bitcast.63, bf16[2048,4096]{1,0:T(8,128)(2,1)S(1)} %bitcast.60), kind=kOutput, calls=%fused_computation.10 | convolution fusion | flops 2148007936 | bytes 18350080 | tf_op jit(solution)/shard_map/dot_general | solution.py:450
  55.3 0.0 reduce-scatter.2.cloned.1.call-update
  55.3 1.1 slice_convert_fusion
  56.4 0.2 copy.49
  56.6 26.3 %reduce-scatter.2.cloned.1.call-done = bf16[1024,128]{0,1:T(8,128)(2,1)} async-done(((bf16[4096,128]{0,1:T(8,128)(2,1)}), bf16[1024,128]{0,1:T(8,128)(2,1)}) %reduce-scatter.2.cloned.1.call-update) | async-done | bytes 262160 | tf_op jit(solution)/shard_map/reduce_scatter | solution.py:449
  82.9 0.0 copy-done.4
  82.9 0.0 copy-done.7
  82.9 1.8 multiply_reduce_fusion
  84.7 0.6 broadcast_in_dim.51.refs_1_
  85.3 50.5 %shard_map.119 = (bf16[1024,4096]{1,0:T(8,128)(2,1)}, f32[256,128]{1,0:T(8,128)}) custom-call(bf16[128,1024]{1,0:T(8,128)(2,1)} %get-tuple-element.10.refs_0_, f32[8,128]{1,0:T(8,128)} %broadcast_in_dim.51.refs_1_), custom_call_target="tpu_custom_call" | custom-call | tf_op jit(solution)/shard_map/pallas_call | solution.py:188
  135.7 0.9 slice_reduce_fusion
  136.7 24.5 %broadcast_multiply_fusion = f32[1024,2,2,512]{3,0,2,1:T(8,128)} fusion(f32[1024]{0:T(1024)S(1)} %rsqrt_bitcast_fusion, bf16[2,4096,2,512]{3,2,1,0:T(2,128)(2,1)} %param.19, bf16[1024,4096]{1,0:T(8,128)(2,1)} %get-tuple-element.7), kind=kOutput, calls=%fused_computation.18 | convolution fusion | flops 17181966336 | bytes 33558528 | tf_op jit(solution)/shard_map/td,edgf->tegf/dot_general | solution.py:372
  161.1 0.0 copy-start.1
  161.1 14.3 %bitcast_convert_fusion.sums_ref = bf16[1024,4096]{1,0:T(8,128)(2,1)S(1)} fusion(bf16[2,512,4096]{2,1,0:T(8,128)(2,1)} %param.20, f32[1024,2,2,512]{3,0,2,1:T(8,128)} %broadcast_multiply_fusion, f32[1024,2]{0,1:T(2,128)S(1)} %constant_dynamic-slice_fusion), kind=kOutput, calls=%fused_computation | convolution fusion | flops 8601468928 | bytes 25174016 | tf_op jit(solution)/shard_map/dot_general | solution.py:376
  175.5 0.0 copy-start.5
  175.5 42.7 %shard_map.120 = f32[128,1024]{1,0:T(8,128)S(1)} custom-call(bf16[1024,4096]{1,0:T(8,128)(2,1)S(1)} %bitcast_convert_fusion.sums_ref), custom_call_target="tpu_custom_call" | custom-call | tf_op jit(solution)/shard_map/pallas_call | solution.py:333
  218.2 0.0 copy-done.5
  218.2 0.8 add_convert_fusion
  219.0 0.0 copy-done.1
  (9 shorter events, 0.1 us)
Async XLA Ops:
  6.5 31.0 %copy-start = (bf16[16,512,128]{2,1,0:T(8,128)(2,1)S(1)}, bf16[16,512,128]{2,1,0:T(8,128)(2,1)}, u32[]{:S(2)}) copy-start(bf16[16,512,128]{2,1,0:T(8,128)(2,1)} %param.14) | copy-start | bytes 6291460
  6.5 76.3 %reduce-scatter.2.cloned.1.call-start = ((), (), s32[]{:S(2)}) async-start(), calls=%async_computation.1 | async-start | bytes 1310720 | tf_op jit(solution)/shard_map/reduce_scatter | solution.py:449
  15.8 22.9 %copy-start.6 = (s32[1024]{0:T(1024)S(1)}, s32[1024]{0:T(1024)}, u32[]{:S(2)}) copy-start(s32[1024]{0:T(1024)} %convert_reduce_fusion) | copy-start | bytes 12292
  37.6 1.3 copy-start.3
  43.0 8.5 %slice-start = ((s8[16777216]{0:T(1024)(128)(4,1)}), s8[4194304]{0:T(1024)(128)(4,1)S(1)}, s32[]{:S(2)}) async-start(s8[16777216]{0:T(1024)(128)(4,1)} %bitcast.59), calls=%async_computation.2 | async-start | bytes 8388608
  46.6 4.0 %copy-start.2 = (bf16[16,512,128]{2,1,0:T(8,128)(2,1)S(1)}, bf16[16,512,128]{2,1,0:T(8,128)(2,1)}, u32[]{:S(2)}) copy-start(bf16[16,512,128]{2,1,0:T(8,128)(2,1)} %param.15) | copy-start | bytes 6291460
  46.6 4.8 %slice-start.1 = ((s8[16777216]{0:T(1024)(128)(4,1)}), s8[4194304]{0:T(1024)(128)(4,1)S(1)}, s32[]{:S(2)}) async-start(s8[16777216]{0:T(1024)(128)(4,1)} %bitcast.59), calls=%async_computation.3 | async-start | bytes 8388608
  46.6 4.8 %slice-start.2 = ((s8[16777216]{0:T(1024)(128)(4,1)}), s8[4194304]{0:T(1024)(128)(4,1)S(1)}, s32[]{:S(2)}) async-start(s8[16777216]{0:T(1024)(128)(4,1)} %bitcast.59), calls=%async_computation.4 | async-start | bytes 8388608
  46.7 5.3 %slice-start.3 = ((s8[16777216]{0:T(1024)(128)(4,1)}), s8[4194304]{0:T(1024)(128)(4,1)S(1)}, s32[]{:S(2)}) async-start(s8[16777216]{0:T(1024)(128)(4,1)} %bitcast.59), calls=%async_computation.5 | async-start | bytes 8388608
  51.9 31.0 %copy-start.4 = (bf16[128,1024]{1,0:T(8,128)(2,1)S(1)}, bf16[128,1024]{1,0:T(8,128)(2,1)}, u32[]{:S(2)}) copy-start(bf16[128,1024]{1,0:T(8,128)(2,1)} %param.17) | copy-start | bytes 786436
  51.9 31.0 %copy-start.7 = (f32[1024]{0:T(1024)S(1)}, f32[1024]{0:T(1024)}, u32[]{:S(2)}) copy-start(f32[1024]{0:T(1024)} %param.18) | copy-start | bytes 12292
  161.1 57.9 %copy-start.1 = (bf16[16,512,128]{2,1,0:T(8,128)(2,1)S(1)}, bf16[16,512,128]{2,1,0:T(8,128)(2,1)}, u32[]{:S(2)}) copy-start(bf16[16,512,128]{2,1,0:T(8,128)(2,1)} %param.14) | copy-start | bytes 6291460
  175.5 42.7 %copy-start.5 = (bf16[1024,128]{0,1:T(8,128)(2,1)S(1)}, bf16[1024,128]{0,1:T(8,128)(2,1)}, u32[]{:S(2)}) copy-start(bf16[1024,128]{0,1:T(8,128)(2,1)} %reduce-scatter.2.cloned.1.call-done) | copy-start | bytes 786436
Sparse Core Ops, SparseCore 0:
  55.4 27.4 reduce-scatter.1

commit v3 on v2

--- a/solution.py
+++ b/solution.py
@@ -59,8 +59,8 @@
 
 def gather_kernel(chips, count_exp, with_extra, *refs):
     if with_extra:
-        own_ref, extra_ref, out_ref, extra_out = refs[:4]
-        refs = refs[4:]
+        own_ref, extra_ref, weight_ref, product_ref, extra_out, out_ref, weight, weight_sem = refs[:8]
+        refs = refs[8:]
     else:
         own_ref, out_ref = refs[:2]
         extra_ref = extra_out = None
@@ -103,6 +103,36 @@
         copy.start()
         started.append(copy)
         return copy
+
+    loads = {}
+    if with_extra:
+        for chunk in by_distance(count_exp):
+            first = lax.rem(exp - chunk + count_exp, count_exp) * cols
+            loads[chunk] = pltpu.make_async_copy(
+                weight_ref.at[pl.ds(pl.multiple_of(first, cols), cols)],
+                weight.at[chunk],
+                weight_sem.at[chunk],
+            )
+
+    def multiply(chunk):
+        loads[chunk].wait()
+        for copy in sib_of[chunk]:
+            copy.wait_recv()
+        first = lax.rem(exp - chunk + count_exp, count_exp) * cols
+        chosen = pl.ds(pl.multiple_of(first, cols), cols)
+        tall, wide = 512, 256
+        across_tiles = product_ref.shape[1] // wide
+
+        def tile(at, carry):
+            down = pl.ds(pl.multiple_of(at // across_tiles * tall, tall), tall)
+            side = pl.ds(pl.multiple_of(lax.rem(at, across_tiles) * wide, wide), wide)
+            product = jnp.dot(
+                out_ref[down, chosen], weight[chunk, :, side], preferred_element_type=jnp.float32
+            )
+            product_ref[down, side] = product if chunk == 0 else product_ref[down, side] + product
+            return carry
+
+        lax.fori_loop(0, product_ref.shape[0] // tall * across_tiles, tile, 0)
 
     keeps = [pltpu.make_async_copy(own_ref, block(ctx, 0, None), local_sem.at[0])]
     if with_extra:
@@ -118,15 +148,17 @@
             )
     for step in by_distance(count_exp)[1:]:
         arriving[step] = send(own_ref, block(ctx, 0, None), z_sems, step, across[step])
+    for chunk in loads:
+        loads[chunk].start()
     for keep in keeps:
         keep.wait()
 
     ring_sems, sib_sems = (ring_send, ring_recv), (sib_send, sib_recv)
-    ring, sib = {}, []
+    ring, sib_of = {}, {chunk: [] for chunk in chunks}
 
     def share(owner, chunk, part, at):
         piece = block(owner, chunk, part)
-        sib.append(send(piece, piece, sib_sems, at, sibling))
+        sib_of[chunk].append(send(piece, piece, sib_sems, at, sibling))
 
     def hop_on(chunk, hop, side):
         if chunk == "extra" and hop == half and side == 1:
@@ -152,7 +184,7 @@
             at = len(chunks) + (side * half + hop - 1) * len(chunks) + slot_of[chunk]
             share(source, chunk, part, at)
 
-    for turn in range(len(chunks) + half):
+    for turn in range(len(chunks) + half + 1):
         if turn < len(chunks):
             chunk = chunks[turn]
             if chunk == "extra":
@@ -166,31 +198,45 @@
         for hop in range(1, half + 1):
             if 0 <= turn - hop < len(chunks):
                 arrive(chunks[turn - hop], hop)
-    for copy in sib:
-        copy.wait_recv()
+        done = turn - half - 1
+        if 0 <= done < len(chunks) and chunks[done] in loads:
+            multiply(chunks[done])
+    for chunk in chunks:
+        if chunk not in loads:
+            for copy in sib_of[chunk]:
+                copy.wait_recv()
     for copy in started:
         copy.wait_send()
 
 
-def gather(count_ctx, count_exp, own, extra, collective_id):
+def gather(count_ctx, count_exp, own, extra, weight, collective_id):
     chips = count_ctx // 2
     half = chips // 2
     rows, cols = own.shape
     outs = [jax.ShapeDtypeStruct((count_ctx * rows, count_exp * cols), own.dtype)]
     operands = [own]
+    place, space, held = pl.ANY, None, []
+    dma = pltpu.SemaphoreType.DMA
     if extra is not None:
-        operands.append(extra)
+        operands += [extra, weight]
+        held = [
+            pltpu.VMEM(outs[0].shape, own.dtype),
+            pltpu.VMEM((count_exp, cols, weight.shape[1]), weight.dtype),
+            dma((count_exp,)),
+        ]
+        outs = [jax.ShapeDtypeStruct((count_ctx * rows, weight.shape[1]), jnp.float32)]
+        place, space = pltpu.VMEM, 52 * 1024 * 1024
         outs.append(
             jax.ShapeDtypeStruct((count_ctx * count_exp * extra.shape[0], extra.shape[1]), extra.dtype)
         )
-    chunks = count_exp + len(operands) - 1
-    dma = pltpu.SemaphoreType.DMA
+    chunks = count_exp + len(outs) - 1
     result = pl.pallas_call(
         functools.partial(gather_kernel, chips, count_exp, extra is not None),
         out_shape=outs,
         in_specs=[pl.BlockSpec(memory_space=pl.ANY)] * len(operands),
-        out_specs=[pl.BlockSpec(memory_space=pl.ANY)] * len(outs),
+        out_specs=[pl.BlockSpec(memory_space=place)] + [pl.BlockSpec(memory_space=pl.ANY)] * (len(outs) - 1),
         scratch_shapes=[
+            *held,
             dma((2,)),
             dma((2 * count_exp,)),
             dma((2 * count_exp,)),
@@ -199,13 +245,15 @@
             dma(((2 * half + 1) * chunks,)),
             dma(((2 * half + 1) * chunks,)),
         ],
-        compiler_params=pltpu.CompilerParams(collective_id=collective_id, has_side_effects=True),
+        compiler_params=pltpu.CompilerParams(
+            collective_id=collective_id, has_side_effects=True, vmem_limit_bytes=space
+        ),
     )(*operands)
     return result if extra is not None else result[0]
 
 
 def scatter_kernel(
-    chips, count_exp, sums_ref, out_ref, held, passed, landed, leaving, returned,
+    chips, count_exp, rows_ref, weight_ref, out_ref, weight, held, passed, landed, leaving, returned,
     load_sem, sib_send, sib_recv, ring_send, ring_recv, z_send, z_recv,
 ):
     ctx, exp, core, place, sibling, sides, across = neighbours(chips, count_exp)
@@ -215,11 +263,7 @@
     greet([*across[1:], *sides, sibling])
 
     def block(owner, chunk):
-        column = across[chunk][1] * cols
-        return sums_ref.at[
-            pl.ds(pl.multiple_of(owner * rows, rows), rows),
-            pl.ds(pl.multiple_of(column, cols), cols),
-        ]
+        return held.at[chunk, pl.ds(pl.multiple_of(owner * rows, rows), rows)]
 
     started = []
 
@@ -239,23 +283,41 @@
     loads, swaps = {}, {}
     offsets = sorted(range(chips), key=lambda offset: -min(offset, chips - offset))
     for chunk in order:
+        column = pl.ds(pl.multiple_of(across[chunk][1] * cols, cols), cols)
+        loads[chunk] = pltpu.make_async_copy(
+            weight_ref.at[:, column], weight.at[chunk], load_sem.at[chunk]
+        )
+        loads[chunk].start()
+
+    def multiply(chunk):
+        loads[chunk].wait()
+        tall, wide = 512, 256
+        across_tiles = cols // wide
+
+        def tile(at, carry):
+            down = pl.ds(pl.multiple_of(at // across_tiles * tall, tall), tall)
+            side = pl.ds(pl.multiple_of(lax.rem(at, across_tiles) * wide, wide), wide)
+            held[chunk, down, side] = jnp.dot(
+                rows_ref[down], weight[chunk, :, side], preferred_element_type=jnp.float32
+            ).astype(held.dtype)
+            return carry
+
+        lax.fori_loop(0, rows_ref.shape[0] // tall * across_tiles, tile, 0)
         for offset in offsets:
             at = offset * count_exp + chunk
             theirs = ring_member(place + offset, chips, 1 - core)
-            mine = ring_member(place + offset, chips, core)
             swaps[offset, chunk] = send(
                 block(theirs, chunk), passed.at[at], (sib_send, sib_recv), at, sibling
             )
-            loads[offset, chunk] = pltpu.make_async_copy(
-                block(mine, chunk), held.at[at], load_sem.at[at]
-            )
-            loads[offset, chunk].start()
+
+    def mine(offset):
+        return pl.multiple_of(ring_member(place + offset, chips, core) * rows, rows)
 
     def pair(offset, chunk):
-        loads[offset, chunk].wait()
         swaps[offset, chunk].wait_recv()
         at = offset * count_exp + chunk
-        return held[at].astype(jnp.float32) + passed[at].astype(jnp.float32)
+        ours = held[chunk, pl.ds(mine(offset), rows)]
+        return ours.astype(jnp.float32) + passed[at].astype(jnp.float32)
 
     ring = {}
     stretch = rows // 2
@@ -264,17 +326,14 @@
         return (side * half + step - 1) * count_exp + chunk
 
     def pass_on(offset, side, step, chunk):
-        at = offset * count_exp + chunk
         slot = ring_slot(side, step, chunk)
-        source, target = held.at[at], landed.at[slot]
-        if step == 1:
-            source = source.at[pl.ds(side * stretch, stretch)]
-            target = target.at[pl.ds(side * stretch, stretch)]
+        start, height = (side * stretch, stretch) if step == 1 else (0, rows)
+        source = held.at[chunk, pl.ds(pl.multiple_of(mine(offset) + start, stretch), height)]
+        target = landed.at[slot, pl.ds(start, height)]
         ring[side, step, chunk] = send(source, target, (ring_send, ring_recv), slot, sides[side])
 
     def begin(chunk):
-        at = half * count_exp + chunk
-        held[at] = pair(half, chunk).astype(held.dtype)
+        held[chunk, pl.ds(mine(half), rows)] = pair(half, chunk).astype(held.dtype)
         for side in range(2):
             pass_on(half, side, 1, chunk)
 
@@ -282,14 +341,19 @@
         for side in range(2):
             offset = half - step + 1
             offset = offset if side == 0 else chips - offset
-            at = offset * count_exp + chunk
-            held[at] = pair(offset, chunk).astype(held.dtype)
+            total = pair(offset, chunk)
             ring[side, step - 1, chunk].wait_recv()
             slot = ring_slot(side, step - 1, chunk)
-            part = pl.ds(side * stretch, stretch) if step == 2 else pl.ds(0, rows)
-            held[at, part] = (
-                held[at, part].astype(jnp.float32) + landed[slot, part].astype(jnp.float32)
-            ).astype(held.dtype)
+            if step == 2:
+                came = landed[slot, pl.ds(side * stretch, stretch)].astype(jnp.float32)
+                parts = [total[:stretch], total[stretch:]]
+                parts[side] = parts[side] + came
+                for which in range(2):
+                    down = pl.ds(pl.multiple_of(mine(offset) + which * stretch, stretch), stretch)
+                    held[chunk, down] = parts[which].astype(held.dtype)
+            else:
+                total = total + landed[slot].astype(jnp.float32)
+                held[chunk, pl.ds(mine(offset), rows)] = total.astype(held.dtype)
             pass_on(offset, side, step, chunk)
 
     back = {}
@@ -307,7 +371,10 @@
                 leaving.at[chunk], returned.at[chunk], (z_send, z_recv), chunk, across[chunk]
             )
 
+    multiply(order[0])
     for turn in range(count_exp + half):
+        if turn + 1 < count_exp:
+            multiply(order[turn + 1])
         if turn < count_exp:
             begin(order[turn])
         for step in range(2, half + 1):
@@ -324,24 +391,26 @@
         copy.wait_send()
 
 
-def scatter(count_ctx, count_exp, sums, collective_id):
+def scatter(count_ctx, count_exp, rows_in, weight, collective_id):
     chips = count_ctx // 2
     half = chips // 2
-    rows, cols = sums.shape[0] // count_ctx, sums.shape[1] // count_exp
+    rows, cols = rows_in.shape[0] // count_ctx, weight.shape[1] // count_exp
     dma = pltpu.SemaphoreType.DMA
     blocks, hops = chips * count_exp, 2 * half * count_exp
+    kind = rows_in.dtype
     return pl.pallas_call(
         functools.partial(scatter_kernel, chips, count_exp),
         out_shape=jax.ShapeDtypeStruct((rows, cols), jnp.float32),
-        in_specs=[pl.BlockSpec(memory_space=pl.ANY)],
+        in_specs=[pl.BlockSpec(memory_space=pltpu.VMEM), pl.BlockSpec(memory_space=pl.ANY)],
         out_specs=pl.BlockSpec(memory_space=pltpu.VMEM),
         scratch_shapes=[
-            pltpu.VMEM((blocks, rows, cols), sums.dtype),
-            pltpu.VMEM((blocks, rows, cols), sums.dtype),
-            pltpu.VMEM((hops, rows, cols), sums.dtype),
-            pltpu.VMEM((count_exp, rows, cols), sums.dtype),
-            pltpu.VMEM((count_exp, rows, cols), sums.dtype),
-            dma((blocks,)),
+            pltpu.VMEM((count_exp, weight.shape[0], cols), kind),
+            pltpu.VMEM((count_exp, rows_in.shape[0], cols), kind),
+            pltpu.VMEM((blocks, rows, cols), kind),
+            pltpu.VMEM((hops, rows, cols), kind),
+            pltpu.VMEM((count_exp, rows, cols), kind),
+            pltpu.VMEM((count_exp, rows, cols), kind),
+            dma((count_exp,)),
             dma((blocks,)),
             dma((blocks,)),
             dma((hops,)),
@@ -350,9 +419,9 @@
             dma((count_exp,)),
         ],
         compiler_params=pltpu.CompilerParams(
-            collective_id=collective_id, has_side_effects=True, vmem_limit_bytes=40 * 1024 * 1024
+            collective_id=collective_id, has_side_effects=True, vmem_limit_bytes=52 * 1024 * 1024
         ),
-    )(sums)
+    )(rows_in, weight)
 
 
 def three_terms(values):
@@ -367,15 +436,11 @@
     return jnp.sum(jnp.where(hit, gate_weights[:, :, None], 0.0), axis=1)
 
 
-def expert_mlp(rows, inverse, gates, w_in, w_out):
-    experts, _, _, units = w_in.shape
-    hidden_pre = jnp.einsum("td,edgf->tegf", rows, w_in, preferred_element_type=jnp.float32)
-    hidden_pre = hidden_pre * inverse[:, None, None, None]
-    activated = jax.nn.silu(hidden_pre[:, :, 0, :]) * hidden_pre[:, :, 1, :] * gates[:, :, None]
-    activated = activated.astype(jnp.bfloat16).reshape(rows.shape[0], experts * units)
-    return jnp.dot(
-        activated, w_out.reshape(experts * units, w_out.shape[2]), preferred_element_type=jnp.float32
-    ).astype(jnp.bfloat16)
+def activate(hidden_pre, inverse, gates):
+    tokens, experts = gates.shape
+    hidden_pre = (hidden_pre * inverse[:, None]).reshape(tokens, experts, 2, -1)
+    activated = jax.nn.silu(hidden_pre[:, :, 0]) * hidden_pre[:, :, 1] * gates[:, :, None]
+    return activated.astype(jnp.bfloat16).reshape(tokens, -1)
 
 
 def body(
@@ -419,7 +484,7 @@
     packed = jnp.concatenate(
         [latent, *own_gates, jnp.zeros((tokens, spare), jnp.bfloat16)], axis=1
     )
-    packed = gather(count_ctx, 1, packed, None, 0)
+    packed = gather(count_ctx, 1, packed, None, None, 0)
     piece = packed[:, :width]
     all_gates = jnp.sum(
         packed[:, width : width + 3 * experts].astype(jnp.float32).reshape(-1, 3, experts), axis=1
@@ -457,12 +522,18 @@
     hidden = residual.astype(jnp.float32) + attn_t.T
     squares = jnp.sum(hidden * hidden, axis=1)
     scaled = (hidden * norm_gain[None, :]).astype(jnp.bfloat16)
-    rows, squares = gather(
-        count_ctx, count_exp, scaled, jnp.broadcast_to(squares[None, :], (8, tokens)), 1
+    hidden_pre, squares = gather(
+        count_ctx,
+        count_exp,
+        scaled,
+        jnp.broadcast_to(squares[None, :], (8, tokens)),
+        jnp.transpose(w_in, (1, 0, 2, 3)).reshape(w_in.shape[1], -1),
+        1,
     )
     squares = jnp.sum(squares.reshape(count_ctx, count_exp, 8, tokens)[:, :, 0], axis=1)
     inverse = lax.rsqrt(squares.reshape(-1) / D + epsilon)
-    mixed = scatter(count_ctx, count_exp, expert_mlp(rows, inverse, gates, w_in, w_out), 2)
+    activated = activate(hidden_pre, inverse, gates)
+    mixed = scatter(count_ctx, count_exp, activated, w_out.reshape(-1, w_out.shape[2]), 2)
     return (hidden + mixed).astype(jnp.bfloat16)
 
 

time: 226 us -> 291 us (1.29); the launches traced: 226 us -> 286 us
  local copies, waits for them, and re-layouts: 9.35 us -> 99 us
  matrix products: 51.7 us -> 14.3 us
  waiting for transfers between devices: 26.3 us -> 0.02 us
  Pallas kernels: 113 us -> 138 us
  other arithmetic: 11.6 us -> 20.1 us
    reshape x0 -> x2, local copies, waits for them, and re-layouts: none -> 39.4 us  [the longest x1 27.7 us: body(): jnp.transpose(w_in, (1, 0, 2, 3)).reshape(w_in.shape[1], -1)]
    dot_general x2 -> x0, matrix products: 38.8 us -> none  [the longest x1 24.5 us: expert_mlp(): jnp.einsum('td,edgf->tegf', rows, w_in, preferred_element_type=jnp.float32)]
    slice x0 -> x1, local copies, waits for them, and re-layouts: none -> 30.5 us  [activate(): hidden_pre[:, :, 0]]
    reduce_scatter x1, waiting for transfers between devices: 26.3 us -> 0.01 us  [body(): lax.psum_scatter(lax.dot_general(w_o, head_out, (((0,), (1,)), ((), ())),...]
    pallas_call x2, Pallas kernels: 70.5 us -> 85.5 us  [gather(): pl.pallas_call(functools.partial(gather_kernel, chips, count_exp, extra i...]
    transpose x0 -> x1, local copies, waits for them, and re-layouts: none -> 14.4 us  [body(): jnp.transpose(w_in, (1, 0, 2, 3)).reshape(w_in.shape[1], -1)]
    pallas_call x1, Pallas kernels: 42.7 us -> 52.7 us  [scatter(): pl.pallas_call(functools.partial(scatter_kernel, chips, count_exp), out_s...]
    mul x0 -> x1, other arithmetic: none -> 7.21 us  [activate(): hidden_pre = (hidden_pre * inverse[:, None]).reshape(tokens, experts, 2, -1)]
  transfers between devices with their start and end apart: 1 -> 1, of which waited for: 1 -> 0; matrix products, arithmetic and copies ran while one was open for 1% -> 16% of each run, Pallas kernels for 0% -> 0%
where the time goes in v3:
time: 291 us; the launch traced here: 286 us
  Pallas kernels  138 us (47%)
  local copies, waits for them, and re-layouts  99 us (34%)
  other arithmetic  20.1 us (7%)
  matrix products  14.3 us (5%)
  between operations  14.2 us (5%)
    pallas_call x2, Pallas kernels, gather(): pl.pallas_call(functools.partial(gather_kernel, chips, count_exp, extra i...  85.5 us
    pallas_call x1, Pallas kernels, scatter(): pl.pallas_call(functools.partial(scatter_kernel, chips, count_exp), out_s...  52.7 us
    slice x1, local copies, waits for them, and re-layouts, activate(): hidden_pre[:, :, 0]  30.5 us
    reshape x1, local copies, waits for them, and re-layouts, body(): jnp.transpose(w_in, (1, 0, 2, 3)).reshape(w_in.shape[1], -1)  27.7 us
    transpose x1, local copies, waits for them, and re-layouts, body(): jnp.transpose(w_in, (1, 0, 2, 3)).reshape(w_in.shape[1], -1)  14.4 us
    reshape x1, local copies, waits for them, and re-layouts, activate(): hidden_pre = (hidden_pre * inverse[:, None]).reshape(tokens, experts, 2, -1)  11.7 us
    unnamed x30, local copies, waits for them, and re-layouts  11.7 us
    mul x1, other arithmetic, activate(): hidden_pre = (hidden_pre * inverse[:, None]).reshape(tokens, experts, 2, -1)  7.21 us
  transfers between devices with their start and end apart: 1, of which 0 were waited for; matrix products, arithmetic and copies ran while one was open for 16% of the time, Pallas kernels for 0%

profile of v3, /device:TPU:0, one launch (start us, length us, event | category | flops | bytes accessed | tf_op | source)
XLA Modules:
  0.0 285.7 jit_solution(9397514308756239898)
XLA Ops:
  6.5 0.0 copy-start
  6.5 0.0 reduce-scatter.2.cloned.1.call-start
  6.5 0.9 select_reduce_fusion
  7.4 0.1 copy.58
  7.5 0.1 copy.59
  7.6 0.1 copy.61
  7.7 1.1 copy.60
  8.8 0.8 concatenate.7.refs_0_
  9.6 20.1 %shard_map.118 = bf16[1024,640]{1,0:T(8,128)(2,1)} custom-call(bf16[128,640]{1,0:T(8,128)(2,1)} %concatenate.7.refs_0_), custom_call_target="tpu_custom_call" | custom-call | tf_op jit(solution)/shard_map/pallas_call | solution.py:233
  29.7 0.8 reduce-window.8
  30.6 0.1 convert_reduce_fusion
  30.7 0.1 convert_reduce_fusion.1
  30.7 1.5 copy.55
  32.3 0.0 copy-done
  32.3 2.1 convolution_convert_fusion.1
  34.4 0.0 copy-start.4
  34.4 0.3 copy.70
  34.7 2.0 pad_maximum_fusion
  36.7 0.0 copy-done.4
  36.7 4.1 %fusion.1 = (f32[2048]{0:T(1024)S(1)}, f32[2048,1024]{0,1:T(8,128)S(1)}) fusion(s32[2048]{0:T(1024)S(1)} %get-tuple-element.19, s32[2048]{0:T(1024)S(1)} %get-tuple-element.20, s32[1024]{0:T(1024)S(1)} %convert_reduce_fusion, bf16[2048,576]{1,0:T(8,128)(2,1)S(1)} %bitcast.55, bf16[1024,640]{1,0:T(8,128)(2,1)S(1)} %copy-done.4), kind=kOutput, calls=%fused_computation.4 | convolution fusion | flops 2428499968 | bytes 12087296 | tf_op jit(solution)/shard_map/dot_general | solution.py:498
  40.8 0.0 slice-start
  40.8 3.6 %fusion.3 = f32[2048]{0:T(1024)S(1)} fusion(f32[2048,1024]{0,1:T(8,128)S(1)} %get-tuple-element.18, f32[2048]{0:T(1024)S(1)} %broadcast_maximum_fusion, s32[2048]{0:T(1024)S(1)} %get-tuple-element.19, s32[2048]{0:T(1024)S(1)} %get-tuple-element.20, s32[1024]{0:T(1024)S(1)} %convert_reduce_fusion), kind=kLoop, calls=%fused_computation.7 | loop fusion | flops 16775168 | bytes 8425472 | tf_op jit(solution)/shard_map/reduce_sum | solution.py:502
  44.4 0.0 copy-start.3
  44.4 0.0 slice-start.1
  44.5 0.0 slice-start.2
  44.5 0.0 slice-start.3
  44.5 4.0 %divide_convert_fusion = bf16[2048,512]{1,0:T(8,128)(2,1)S(1)} fusion(f32[2048]{0:T(1024)S(1)} %fusion.3, f32[2048,1024]{0,1:T(8,128)S(1)} %get-tuple-element.18, f32[2048]{0:T(1024)S(1)} %broadcast_maximum_fusion, s32[2048]{0:T(1024)S(1)} %get-tuple-element.19, s32[2048]{0:T(1024)S(1)} %get-tuple-element.20, s32[1024]{0:T(1024)S(1)} %convert_reduce_fusion, ...), kind=kOutput, calls=%fused_computation.13 | convolution fusion | flops 2166358016 | bytes 11571200 | tf_op jit(solution)/shard_map/dot_general | solution.py:503
  48.5 0.0 copy-done.3
  48.5 0.8 convolution_convert_fusion.2
  49.2 0.0 slice-done
  49.3 0.0 slice-done.1
  49.3 0.0 slice-done.2
  49.3 0.5 slice-done.3
  49.7 3.4 %fusion.2 = bf16[4096,128]{0,1:T(8,128)(2,1)} fusion(bf16[128,2048]{0,1:T(8,128)(2,1)S(1)} %bitcast.54, bf16[2048,4096]{1,0:T(8,128)(2,1)S(1)} %bitcast.43), kind=kOutput, calls=%fused_computation.6 | convolution fusion | flops 2148007936 | bytes 18350080 | tf_op jit(solution)/shard_map/dot_general | solution.py:515
  53.1 0.0 reduce-scatter.2.cloned.1.call-update
  53.1 14.4 %copy.63 = bf16[4096,2,2,512]{3,2,1,0:T(2,128)(2,1)} copy(bf16[4096,2,2,512]{3,2,0,1:T(2,128)(2,1)} %bitcast.47) | data formatting | bytes 33554432 | tf_op jit(solution)/shard_map/transpose | solution.py:530
  67.5 27.7 %reshape.98.refs_2_ = bf16[4096,2048]{1,0:T(8,128)(2,1)} reshape(bf16[4096,2,2,512]{3,2,1,0:T(2,128)(2,1)} %copy.63) | data formatting | bytes 33554432 | tf_op jit(solution)/shard_map/reshape | solution.py:530
  95.2 0.1 slice_convert_fusion
  95.3 0.2 copy.66
  95.6 0.2 copy.67
  95.8 1.4 mul.62
  97.2 0.0 copy-start.5
  97.2 0.0 copy-start.7
  97.2 3.0 %copy.75 = f32[128,8,2,512]{3,1,2,0:T(8,128)} copy(f32[128,8,2,512]{3,2,1,0:T(2,128)S(1)} %bitcast.48) | data formatting | bytes 8388608
  100.2 0.0 reduce-scatter.2.cloned.1.call-done
  100.2 0.0 copy-done.5
  100.2 0.0 copy-done.7
  100.2 1.1 multiply_reduce_fusion
  101.4 65.5 %shard_map.119 = (f32[1024,2048]{1,0:T(8,128)}, f32[256,128]{1,0:T(8,128)S(1)}) custom-call(bf16[128,1024]{1,0:T(8,128)(2,1)S(1)} %get-tuple-element.12.refs_0_, f32[8,128]{1,0:T(8,128)S(1)} %broadcast_in_dim.51.refs_1_, bf16[4096,2048]{1,0:T(8,128)(2,1)} %reshape.98.refs_2_), custom_call_target="tpu_custom_call" | custom-call | tf_op jit(solution)/shard_map/pallas_call | solution.py:233
  166.9 7.2 %broadcast_multiply_fusion = f32[1024,2048]{1,0:T(8,128)} fusion(f32[1024,2048]{1,0:T(8,128)} %get-tuple-element.7, f32[1024]{0:T(1024)S(1)} %rsqrt_bitcast_fusion), kind=kLoop, calls=%fused_computation.12 | loop fusion | flops 2097152 | bytes 16781312 | tf_op jit(solution)/shard_map/mul | solution.py:441
  174.1 11.7 %reshape.100 = f32[1024,2,2,512]{3,2,1,0:T(2,128)} reshape(f32[1024,2048]{1,0:T(8,128)} %broadcast_multiply_fusion) | data formatting | bytes 16777216 | tf_op jit(solution)/shard_map/reshape | solution.py:441
  185.8 30.5 %slice_reduce_fusion.1 = (f32[1024,2,512]{2,1,0:T(2,128)}, f32[1024,2,512]{2,1,0:T(2,128)S(1)}) fusion(f32[1024,2,2,512]{3,2,1,0:T(2,128)} %reshape.100), kind=kLoop, calls=%fused_computation.10 | loop fusion | bytes 16777216 | tf_op jit(solution)/shard_map/slice | solution.py:442
  216.3 3.2 %copy.73 = f32[128,8,2,512]{3,1,2,0:T(8,128)S(1)} copy(f32[128,8,2,512]{3,2,1,0:T(2,128)} %bitcast.50) | data formatting | bytes 8388608
  219.5 0.0 copy-start.2
  219.5 1.0 copy.74
  220.6 1.1 copy-done.2
  221.7 3.2 %multiply_convert_fusion.rows_ref = bf16[1024,1024]{1,0:T(8,128)(2,1)} fusion(f32[1024,1024]{1,0:T(8,128)S(1)} %bitcast.44, f32[1024,1024]{1,0:T(8,128)S(1)} %bitcast.46, f32[1024,1024]{1,0:T(8,128)S(1)} %bitcast.45), kind=kLoop, calls=%fused_computation.11 | loop fusion | flops 7340032 | bytes 14680064 | tf_op jit(solution)/shard_map/convert_element_type | solution.py:443
  224.9 0.0 copy-start.1
  224.9 0.0 copy-start.6
  224.9 52.7 %shard_map.120 = f32[128,1024]{1,0:T(8,128)S(1)} custom-call(bf16[1024,1024]{1,0:T(8,128)(2,1)} %multiply_convert_fusion.rows_ref, bf16[1024,4096]{1,0:T(8,128)(2,1)} %bitcast.51), custom_call_target="tpu_custom_call" | custom-call | tf_op jit(solution)/shard_map/pallas_call | solution.py:401
  277.6 0.0 copy-done.6
  277.6 0.8 add_convert_fusion
  278.4 0.0 copy-done.1
  (13 shorter events, 0.1 us)
Async XLA Ops:
  6.5 25.8 %copy-start = (bf16[16,512,128]{2,1,0:T(8,128)(2,1)S(1)}, bf16[16,512,128]{2,1,0:T(8,128)(2,1)}, u32[]{:S(2)}) copy-start(bf16[16,512,128]{2,1,0:T(8,128)(2,1)} %param.14) | copy-start | bytes 6291460
  6.5 93.7 %reduce-scatter.2.cloned.1.call-start = ((), (), s32[]{:S(2)}) async-start(), calls=%async_computation.1 | async-start | bytes 1310720 | tf_op jit(solution)/shard_map/reduce_scatter | solution.py:514
  34.4 2.3 copy-start.4
  40.8 8.4 %slice-start = ((s8[16777216]{0:T(1024)(128)(4,1)}), s8[4194304]{0:T(1024)(128)(4,1)S(1)}, s32[]{:S(2)}) async-start(s8[16777216]{0:T(1024)(128)(4,1)} %bitcast.42), calls=%async_computation.2 | async-start | bytes 8388608
  44.4 4.0 %copy-start.3 = (bf16[16,512,128]{2,1,0:T(8,128)(2,1)S(1)}, bf16[16,512,128]{2,1,0:T(8,128)(2,1)}, u32[]{:S(2)}) copy-start(bf16[16,512,128]{2,1,0:T(8,128)(2,1)} %param.15) | copy-start | bytes 6291460
  44.4 4.8 %slice-start.1 = ((s8[16777216]{0:T(1024)(128)(4,1)}), s8[4194304]{0:T(1024)(128)(4,1)S(1)}, s32[]{:S(2)}) async-start(s8[16777216]{0:T(1024)(128)(4,1)} %bitcast.42), calls=%async_computation.3 | async-start | bytes 8388608
  44.5 4.8 %slice-start.2 = ((s8[16777216]{0:T(1024)(128)(4,1)}), s8[4194304]{0:T(1024)(128)(4,1)S(1)}, s32[]{:S(2)}) async-start(s8[16777216]{0:T(1024)(128)(4,1)} %bitcast.42), calls=%async_computation.4 | async-start | bytes 8388608
  44.5 5.3 %slice-start.3 = ((s8[16777216]{0:T(1024)(128)(4,1)}), s8[4194304]{0:T(1024)(128)(4,1)S(1)}, s32[]{:S(2)}) async-start(s8[16777216]{0:T(1024)(128)(4,1)} %bitcast.42), calls=%async_computation.5 | async-start | bytes 8388608
  97.2 3.0 %copy-start.5 = (bf16[128,1024]{1,0:T(8,128)(2,1)S(1)}, bf16[128,1024]{1,0:T(8,128)(2,1)}, u32[]{:S(2)}) copy-start(bf16[128,1024]{1,0:T(8,128)(2,1)} %param.17) | copy-start | bytes 786436
  97.2 3.0 %copy-start.7 = (f32[1024]{0:T(1024)S(1)}, f32[1024]{0:T(1024)}, u32[]{:S(2)}) copy-start(f32[1024]{0:T(1024)} %param.18) | copy-start | bytes 12292
  219.5 2.2 copy-start.2
  224.9 53.5 %copy-start.1 = (bf16[16,512,128]{2,1,0:T(8,128)(2,1)S(1)}, bf16[16,512,128]{2,1,0:T(8,128)(2,1)}, u32[]{:S(2)}) copy-start(bf16[16,512,128]{2,1,0:T(8,128)(2,1)} %param.14) | copy-start | bytes 6291460
  224.9 52.7 %copy-start.6 = (bf16[1024,128]{0,1:T(8,128)(2,1)S(1)}, bf16[1024,128]{0,1:T(8,128)(2,1)}, u32[]{:S(2)}) copy-start(bf16[1024,128]{0,1:T(8,128)(2,1)} %reduce-scatter.2.cloned.1.call-done) | copy-start | bytes 786436
Sparse Core Ops, SparseCore 0:
  53.3 27.4 reduce-scatter.1

commit v4 on v3

--- a/solution.py
+++ b/solution.py
@@ -108,14 +108,19 @@
     if with_extra:
         for chunk in by_distance(count_exp):
             first = lax.rem(exp - chunk + count_exp, count_exp) * cols
-            loads[chunk] = pltpu.make_async_copy(
-                weight_ref.at[pl.ds(pl.multiple_of(first, cols), cols)],
-                weight.at[chunk],
-                weight_sem.at[chunk],
-            )
+            halves, experts, _, units = weight_ref.shape
+            loads[chunk] = [
+                pltpu.make_async_copy(
+                    weight_ref.at[at // experts, at % experts, pl.ds(pl.multiple_of(first, cols), cols)],
+                    weight.at[chunk, :, pl.ds(at * units, units)],
+                    weight_sem.at[chunk * halves * experts + at],
+                )
+                for at in range(halves * experts)
+            ]
 
     def multiply(chunk):
-        loads[chunk].wait()
+        for load in loads[chunk]:
+            load.wait()
         for copy in sib_of[chunk]:
             copy.wait_recv()
         first = lax.rem(exp - chunk + count_exp, count_exp) * cols
@@ -149,7 +154,8 @@
     for step in by_distance(count_exp)[1:]:
         arriving[step] = send(own_ref, block(ctx, 0, None), z_sems, step, across[step])
     for chunk in loads:
-        loads[chunk].start()
+        for load in loads[chunk]:
+            load.start()
     for keep in keeps:
         keep.wait()
 
@@ -195,12 +201,14 @@
             for side in range(2):
                 hop_on(chunk, 1, side)
             share(ctx, chunk, None, slot_of[chunk])
-        for hop in range(1, half + 1):
+        for hop in range(1, half):
             if 0 <= turn - hop < len(chunks):
                 arrive(chunks[turn - hop], hop)
         done = turn - half - 1
         if 0 <= done < len(chunks) and chunks[done] in loads:
             multiply(chunks[done])
+        if 0 <= turn - half < len(chunks):
+            arrive(chunks[turn - half], half)
     for chunk in chunks:
         if chunk not in loads:
             for copy in sib_of[chunk]:
@@ -219,12 +227,13 @@
     dma = pltpu.SemaphoreType.DMA
     if extra is not None:
         operands += [extra, weight]
+        wide = weight.shape[0] * weight.shape[1] * weight.shape[3]
         held = [
             pltpu.VMEM(outs[0].shape, own.dtype),
-            pltpu.VMEM((count_exp, cols, weight.shape[1]), weight.dtype),
-            dma((count_exp,)),
+            pltpu.VMEM((count_exp, cols, wide), weight.dtype),
+            dma((count_exp * weight.shape[0] * weight.shape[1],)),
         ]
-        outs = [jax.ShapeDtypeStruct((count_ctx * rows, weight.shape[1]), jnp.float32)]
+        outs = [jax.ShapeDtypeStruct((count_ctx * rows, wide), jnp.float32)]
         place, space = pltpu.VMEM, 52 * 1024 * 1024
         outs.append(
             jax.ShapeDtypeStruct((count_ctx * count_exp * extra.shape[0], extra.shape[1]), extra.dtype)
@@ -437,10 +446,14 @@
 
 
 def activate(hidden_pre, inverse, gates):
-    tokens, experts = gates.shape
-    hidden_pre = (hidden_pre * inverse[:, None]).reshape(tokens, experts, 2, -1)
-    activated = jax.nn.silu(hidden_pre[:, :, 0]) * hidden_pre[:, :, 1] * gates[:, :, None]
-    return activated.astype(jnp.bfloat16).reshape(tokens, -1)
+    width = hidden_pre.shape[1] // 2
+    experts = gates.shape[1]
+    owner = lax.broadcasted_iota(jnp.int32, (1, width), 1) // (width // experts)
+    wide_gates = jnp.zeros((1, width), jnp.float32)
+    for expert in range(experts):
+        wide_gates = jnp.where(owner == expert, gates[:, expert][:, None], wide_gates)
+    gate, up = hidden_pre[:, :width] * inverse[:, None], hidden_pre[:, width:] * inverse[:, None]
+    return (jax.nn.silu(gate) * up * wide_gates).astype(jnp.bfloat16)
 
 
 def body(
@@ -527,7 +540,7 @@
         count_exp,
         scaled,
         jnp.broadcast_to(squares[None, :], (8, tokens)),
-        jnp.transpose(w_in, (1, 0, 2, 3)).reshape(w_in.shape[1], -1),
+        jnp.transpose(w_in, (2, 0, 1, 3)),
         1,
     )
     squares = jnp.sum(squares.reshape(count_ctx, count_exp, 8, tokens)[:, :, 0], axis=1)

time: 291 us -> 220 us (0.76); the launches traced: 286 us -> 220 us
  local copies, waits for them, and re-layouts: 99 us -> 24.7 us
  waiting for transfers between devices: 0.02 us -> 10.3 us
  other arithmetic: 20.1 us -> 15.5 us
  Pallas kernels: 138 us -> 142 us
    reshape x2 -> x0, local copies, waits for them, and re-layouts: 39.4 us -> none  [the longest x1 27.7 us: body(): jnp.transpose(w_in, (1, 0, 2, 3)).reshape(w_in.shape[1], -1)]
    slice x1, local copies, waits for them, and re-layouts: 30.5 us -> 0.02 us  [activate(): gates[:, expert][:, None]]
    transpose x1 -> x0, local copies, waits for them, and re-layouts: 14.4 us -> none  [body(): jnp.transpose(w_in, (1, 0, 2, 3)).reshape(w_in.shape[1], -1)]
    reduce_scatter x1, waiting for transfers between devices: 0.01 us -> 10.3 us  [body(): lax.psum_scatter(lax.dot_general(w_o, head_out, (((0,), (1,)), ((), ())),...]
    unnamed x30 -> x28, local copies, waits for them, and re-layouts: 11.7 us -> 21.2 us
    mul x1 -> x0, other arithmetic: 7.21 us -> none  [activate(): hidden_pre = (hidden_pre * inverse[:, None]).reshape(tokens, experts, 2, -1)]
    pallas_call x1, Pallas kernels: 52.7 us -> 57.6 us  [scatter(): pl.pallas_call(functools.partial(scatter_kernel, chips, count_exp), out_s...]
  transfers between devices with their start and end apart: 1 -> 1, of which waited for: 0 -> 1; matrix products, arithmetic and copies ran while one was open for 16% -> 8% of each run, Pallas kernels for 0% -> 0%
where the time goes in v4:
time: 220 us
  Pallas kernels  142 us (65%)
  local copies, waits for them, and re-layouts  24.7 us (11%)
  other arithmetic  15.5 us (7%)
  between operations  13.7 us (6%)
  matrix products  12.9 us (6%)
  waiting for transfers between devices  10.3 us (5%)
    pallas_call x2, Pallas kernels, gather(): pl.pallas_call(functools.partial(gather_kernel, chips, count_exp, extra i...  84.9 us
    pallas_call x1, Pallas kernels, scatter(): pl.pallas_call(functools.partial(scatter_kernel, chips, count_exp), out_s...  57.6 us
    unnamed x28, local copies, waits for them, and re-layouts  21.2 us
    reduce_scatter x1, waiting for transfers between devices, body(): lax.psum_scatter(lax.dot_general(w_o, head_out, (((0,), (1,)), ((), ())),...  10.3 us
    convert_element_type x1, other arithmetic, activate(): return (jax.nn.silu(gate) * up * wide_gates).astype(jnp.bfloat16)  5.42 us
  transfers between devices with their start and end apart: 1, of which 1 were waited for; matrix products, arithmetic and copies ran while one was open for 8% of the time, Pallas kernels for 0%

profile of v4, /device:TPU:0, one launch (start us, length us, event | category | flops | bytes accessed | tf_op | source)
XLA Modules:
  0.0 219.6 jit_solution(7753917594008189918)
XLA Ops:
  6.5 0.0 copy-start
  6.5 0.0 reduce-scatter.2.cloned.1.call-start
  6.5 0.9 select_reduce_fusion
  7.4 0.1 copy.39
  7.5 0.8 reduce-window.8
  8.4 0.7 convert_reduce_fusion
  9.0 0.1 convert_reduce_fusion.1
  9.1 0.7 copy.42
  9.9 0.1 copy.40
  10.0 1.7 copy.41
  11.7 1.5 copy.36
  13.2 0.7 slice.42
  13.9 1.2 copy.48
  15.1 0.6 fusion.13
  15.8 1.7 concatenate.7.refs_0_
  17.5 20.1 %shard_map.118 = bf16[1024,640]{1,0:T(8,128)(2,1)} custom-call(bf16[128,640]{1,0:T(8,128)(2,1)} %concatenate.7.refs_0_), custom_call_target="tpu_custom_call" | custom-call | tf_op jit(solution)/shard_map/pallas_call | solution.py:242
  37.6 0.0 copy-done
  37.6 0.0 copy-start.3
  37.6 0.0 copy-start.6
  37.6 0.8 convolution_convert_fusion.1
  38.3 0.3 pad_maximum_fusion
  38.6 0.2 copy-done.3
  38.9 0.0 copy-done.6
  38.9 4.1 %fusion.1 = (f32[2048]{0:T(1024)S(1)}, f32[2048,1024]{0,1:T(8,128)S(1)}) fusion(s32[2048]{0:T(1024)S(1)} %get-tuple-element.19, s32[2048]{0:T(1024)S(1)} %get-tuple-element.20, s32[1024]{0:T(1024)S(1)} %copy-done.6, bf16[2048,576]{1,0:T(8,128)(2,1)S(1)} %bitcast.47, bf16[1024,640]{1,0:T(8,128)(2,1)S(1)} %copy-done.3), kind=kOutput, calls=%fused_computation.5 | convolution fusion | flops 2428499968 | bytes 12087296 | tf_op jit(solution)/shard_map/dot_general | solution.py:511
  43.0 0.0 slice-start
  43.0 3.6 %fusion.3 = f32[2048]{0:T(1024)S(1)} fusion(f32[2048,1024]{0,1:T(8,128)S(1)} %get-tuple-element.18, f32[2048]{0:T(1024)S(1)} %broadcast_maximum_fusion, s32[2048]{0:T(1024)S(1)} %get-tuple-element.19, s32[2048]{0:T(1024)S(1)} %get-tuple-element.20, s32[1024]{0:T(1024)S(1)} %copy-done.6), kind=kLoop, calls=%fused_computation.8 | loop fusion | flops 16775168 | bytes 8425472 | tf_op jit(solution)/shard_map/reduce_sum | solution.py:515
  46.6 0.0 copy-start.2
  46.6 0.0 slice-start.1
  46.6 0.0 slice-start.2
  46.7 0.0 slice-start.3
  46.7 3.9 %divide_convert_fusion = bf16[2048,512]{1,0:T(8,128)(2,1)S(1)} fusion(f32[2048]{0:T(1024)S(1)} %fusion.3, f32[2048,1024]{0,1:T(8,128)S(1)} %get-tuple-element.18, f32[2048]{0:T(1024)S(1)} %broadcast_maximum_fusion, s32[2048]{0:T(1024)S(1)} %get-tuple-element.19, s32[2048]{0:T(1024)S(1)} %get-tuple-element.20, s32[1024]{0:T(1024)S(1)} %copy-done.6, ...), kind=kOutput, calls=%fused_computation.11 | convolution fusion | flops 2166358016 | bytes 11571200 | tf_op jit(solution)/shard_map/dot_general | solution.py:516
  50.6 0.0 copy-done.2
  50.6 0.8 convolution_convert_fusion.2
  51.4 0.0 slice-done
  51.4 0.0 slice-done.1
  51.4 0.0 slice-done.2
  51.4 0.5 slice-done.3
  51.9 3.4 %fusion.2 = bf16[4096,128]{0,1:T(8,128)(2,1)} fusion(bf16[128,2048]{0,1:T(8,128)(2,1)S(1)} %bitcast.46, bf16[2048,4096]{1,0:T(8,128)(2,1)S(1)} %bitcast.42), kind=kOutput, calls=%fused_computation.7 | convolution fusion | flops 2148007936 | bytes 18350080 | tf_op jit(solution)/shard_map/dot_general | solution.py:528
  55.3 0.0 reduce-scatter.2.cloned.1.call-update
  55.3 1.1 slice_convert_fusion
  56.4 0.2 copy.45
  56.6 0.0 copy-start.4
  56.6 0.0 copy-start.7
  56.6 15.9 %copy.50 = bf16[2,4096,2,512]{3,1,0,2:T(8,128)(2,1)} copy(bf16[2,4096,2,512]{3,2,1,0:T(2,128)(2,1)} %param.19) | data formatting | bytes 33554432 | tf_op args[7]
  72.6 10.3 %reduce-scatter.2.cloned.1.call-done = bf16[1024,128]{0,1:T(8,128)(2,1)} async-done(((bf16[4096,128]{0,1:T(8,128)(2,1)}), bf16[1024,128]{0,1:T(8,128)(2,1)}) %reduce-scatter.2.cloned.1.call-update) | async-done | bytes 262160 | tf_op jit(solution)/shard_map/reduce_scatter | solution.py:527
  82.9 0.0 copy-done.4
  82.9 0.0 copy-done.7
  82.9 1.1 multiply_reduce_fusion
  84.0 64.8 %shard_map.119 = (f32[1024,2048]{1,0:T(8,128)}, f32[256,128]{1,0:T(8,128)S(1)}) custom-call(bf16[128,1024]{1,0:T(8,128)(2,1)S(1)} %get-tuple-element.10.refs_0_, f32[8,128]{1,0:T(8,128)S(1)} %broadcast_in_dim.96.refs_1_, bf16[2,2,4096,512]{3,2,1,0:T(8,128)(2,1)} %bitcast.40), custom_call_target="tpu_custom_call" | custom-call | tf_op jit(solution)/shard_map/pallas_call | solution.py:242
  148.9 5.4 %multiply_convert_fusion.rows_ref = bf16[1024,1024]{1,0:T(8,128)(2,1)} fusion(f32[1024,2048]{1,0:T(8,128)} %get-tuple-element.7, f32[1024]{0:T(1024)S(1)} %bitcast.52, f32[1024]{0:T(1024)S(1)} %bitcast.51, f32[1024]{0:T(1024)S(1)} %rsqrt_bitcast_fusion, pred[1024]{0:T(1024)(128)(4,1)S(1)} %get-tuple-element.21, pred[1024]{0:T(1024)(128)(4,1)S(1)} %get-tuple-element.22), kind=kLoop, calls=%fused_computation.10 | loop fusion | flops 11534336 | bytes 10500096 | tf_op jit(solution)/shard_map/convert_element_type | solution.py:456
  154.4 0.0 copy-start.1
  154.4 0.0 copy-start.5
  154.4 57.6 %shard_map.120 = f32[128,1024]{1,0:T(8,128)S(1)} custom-call(bf16[1024,1024]{1,0:T(8,128)(2,1)} %multiply_convert_fusion.rows_ref, bf16[1024,4096]{1,0:T(8,128)(2,1)} %bitcast.43), custom_call_target="tpu_custom_call" | custom-call | tf_op jit(solution)/shard_map/pallas_call | solution.py:410
  211.9 0.0 copy-done.5
  211.9 0.8 add_convert_fusion
  212.7 0.0 copy-done.1
  (12 shorter events, 0.1 us)
Async XLA Ops:
  6.5 31.0 %copy-start = (bf16[16,512,128]{2,1,0:T(8,128)(2,1)S(1)}, bf16[16,512,128]{2,1,0:T(8,128)(2,1)}, u32[]{:S(2)}) copy-start(bf16[16,512,128]{2,1,0:T(8,128)(2,1)} %param.14) | copy-start | bytes 6291460
  6.5 76.4 %reduce-scatter.2.cloned.1.call-start = ((), (), s32[]{:S(2)}) async-start(), calls=%async_computation.1 | async-start | bytes 1310720 | tf_op jit(solution)/shard_map/reduce_scatter | solution.py:527
  37.6 1.3 copy-start.3
  37.6 1.3 copy-start.6
  43.0 8.4 %slice-start = ((s8[16777216]{0:T(1024)(128)(4,1)}), s8[4194304]{0:T(1024)(128)(4,1)S(1)}, s32[]{:S(2)}) async-start(s8[16777216]{0:T(1024)(128)(4,1)} %bitcast.41), calls=%async_computation.2 | async-start | bytes 8388608
  46.6 4.0 %copy-start.2 = (bf16[16,512,128]{2,1,0:T(8,128)(2,1)S(1)}, bf16[16,512,128]{2,1,0:T(8,128)(2,1)}, u32[]{:S(2)}) copy-start(bf16[16,512,128]{2,1,0:T(8,128)(2,1)} %param.15) | copy-start | bytes 6291460
  46.6 4.8 %slice-start.1 = ((s8[16777216]{0:T(1024)(128)(4,1)}), s8[4194304]{0:T(1024)(128)(4,1)S(1)}, s32[]{:S(2)}) async-start(s8[16777216]{0:T(1024)(128)(4,1)} %bitcast.41), calls=%async_computation.3 | async-start | bytes 8388608
  46.6 4.8 %slice-start.2 = ((s8[16777216]{0:T(1024)(128)(4,1)}), s8[4194304]{0:T(1024)(128)(4,1)S(1)}, s32[]{:S(2)}) async-start(s8[16777216]{0:T(1024)(128)(4,1)} %bitcast.41), calls=%async_computation.4 | async-start | bytes 8388608
  46.7 5.3 %slice-start.3 = ((s8[16777216]{0:T(1024)(128)(4,1)}), s8[4194304]{0:T(1024)(128)(4,1)S(1)}, s32[]{:S(2)}) async-start(s8[16777216]{0:T(1024)(128)(4,1)} %bitcast.41), calls=%async_computation.5 | async-start | bytes 8388608
  56.6 26.3 %copy-start.4 = (bf16[128,1024]{1,0:T(8,128)(2,1)S(1)}, bf16[128,1024]{1,0:T(8,128)(2,1)}, u32[]{:S(2)}) copy-start(bf16[128,1024]{1,0:T(8,128)(2,1)} %param.17) | copy-start | bytes 786436
  56.6 26.3 %copy-start.7 = (f32[1024]{0:T(1024)S(1)}, f32[1024]{0:T(1024)}, u32[]{:S(2)}) copy-start(f32[1024]{0:T(1024)} %param.18) | copy-start | bytes 12292
  154.4 58.4 %copy-start.1 = (bf16[16,512,128]{2,1,0:T(8,128)(2,1)S(1)}, bf16[16,512,128]{2,1,0:T(8,128)(2,1)}, u32[]{:S(2)}) copy-start(bf16[16,512,128]{2,1,0:T(8,128)(2,1)} %param.14) | copy-start | bytes 6291460
  154.4 57.6 %copy-start.5 = (bf16[1024,128]{0,1:T(8,128)(2,1)S(1)}, bf16[1024,128]{0,1:T(8,128)(2,1)}, u32[]{:S(2)}) copy-start(bf16[1024,128]{0,1:T(8,128)(2,1)} %reduce-scatter.2.cloned.1.call-done) | copy-start | bytes 786436
Sparse Core Ops, SparseCore 0:
  55.4 27.4 reduce-scatter.1
